TPU v7x, 32 devices: a whole 2x2x4 slice. The times are simulated.
32 devices in a mesh: segment: 4 (over y, core), space: 8 (over z, x).
Axes of the slice: x: 2, y: 2, z: 4, core: 2. Of those that a mesh axis runs over, the one named last changes fastest.
Arguments:
- x_in: bfloat16 [2, 16, 16, 256], P(None, 'space'), may hold values from -17 to 17
- out_cotangent: bfloat16 [2, 16, 16, 256], P(None, 'space'), may hold values from -17 to 17, as said below
- timesteps: int32 [2], replicated, may hold values from 0 to 999
- labels: int32 [2], replicated, may hold values from 0 to 999
- time_weight: bfloat16 [128, 512], replicated, may hold values from -0.5 to 0.5
- label_table: bfloat16 [1000, 512], replicated, may hold values from -5 to 5
- conv_weight: bfloat16 [4, 3, 3, 256, 256], P('segment'), may hold values from -0.125 to 0.125
- mod_weight: bfloat16 [4, 512, 512], P('segment'), may hold values from -0.25 to 0.25
- mod_bias: float32 [4, 512], P('segment'), may hold values from -3 to 3
- norm_gain: float32 [4, 256], P('segment'), may hold values from 0.25 to 1.75
Outputs:
- segment_grads: bfloat16 [4, 2, 16, 16, 256], P('segment', None, 'space')
- conv_grad: float32 [4, 2304, 256], P('segment', 'space')
- mod_grad: float32 [4, 512, 512], P('segment')
Inputs may be any that keep to these rules, and one draw needn't show every extreme that they name: `out_cotangent`: cotangent from the layers after the chain.
All inputs are finite; a program needn't handle non-finite values.
Results may differ from a plain program's by a relative error of at most 0.0076.
Values may be sent and summed in bfloat16 or wider, within the bound.
No kernel may reach another device: no remote copies, remote signals or barrier semaphores. Data moves between devices by JAX's collectives and lax.ppermute only.
A program may use at most 64 MiB of HBM per device.

v0:
```python
import functools
import math

import jax
import jax.numpy as jnp
from jax import lax
from jax.experimental import pallas as pl
from jax.experimental.pallas import tpu as pltpu
from jax.sharding import PartitionSpec as P

GROUPS = 32
EPSILON = 1e-05
PAIR = 2
VMEM = pl.BlockSpec(memory_space=pltpu.VMEM)
SMEM = pl.BlockSpec(memory_space=pltpu.SMEM)
ANY = pl.BlockSpec(memory_space=pl.ANY)


def sigmoid(values):
    return 1.0 / (1.0 + jnp.exp(-values))


def over_chunks(count, body):
    if count == 1:
        body(0)
    else:

        def step(i, carry):
            body(i)
            return carry

        lax.fori_loop(0, count, step, 0)


def chunk_start(i, size):
    return 0 if isinstance(i, int) else pl.multiple_of(i * size, size)


def fold_rows(values):
    return jnp.sum(values.reshape(values.shape[0] // 8, 8, values.shape[1]), axis=0)


def column(rows):
    return jnp.sum(rows, axis=0, keepdims=True)


def group_sums(rows, width):
    lanes = lax.broadcasted_iota(jnp.int32, rows.shape, 1)
    size = rows.shape[1]
    step = 1
    while step < width:
        ahead = pltpu.roll(rows, size - step, 1)
        behind = pltpu.roll(rows, step, 1)
        rows = rows + jnp.where((lanes & step) == 0, ahead, behind)
        step *= 2
    return rows


def stack_rows(first, second):
    spot = lax.broadcasted_iota(jnp.int32, (8, first.shape[1]), 0)
    return jnp.where(spot == 0, first, jnp.where(spot == 1, second, 0.0))


class Shape:
    def __init__(self, height, cols, channels, space_count):
        self.cols, self.channels = cols, channels
        self.pixels = height * cols
        self.chunk = cols * max(1, min(self.pixels, 256) // cols)
        self.chunks = self.pixels // self.chunk
        self.width = channels // GROUPS
        self.entries = float(self.pixels * self.width)
        self.padded = self.pixels + 2 * cols
        self.own_rows = height // space_count * cols
        self.slab = 9 * channels // space_count
        self.taps = min(9, (self.slab - 1) // channels + 2)
        self.pack = self.slab + self.own_rows + 8
        self.limit = (12 << 20) + self.pixels * channels * 40


def statistics(sh, x_ref):
    zero = jnp.zeros((8, sh.channels), jnp.float32)

    def add(i, sums):
        part = x_ref[pl.ds(chunk_start(i, sh.chunk), sh.chunk), :].astype(jnp.float32)
        return (sums[0] + fold_rows(part), sums[1] + fold_rows(part * part))

    if sh.chunks == 1:
        one, two = add(0, (zero, zero))
    else:
        one, two = lax.fori_loop(0, sh.chunks, add, (zero, zero))
    total = group_sums(stack_rows(column(one), column(two)), sh.width) / sh.entries
    mean = total[0:1]
    return (mean, lax.rsqrt(total[1:2] - mean * mean + EPSILON))


def clear_edges(sh, padded_ref):
    zero = jnp.zeros((3, sh.cols, sh.channels), padded_ref.dtype)
    padded_ref[:, 0 : sh.cols, :] = zero
    padded_ref[:, sh.pixels + sh.cols : sh.padded, :] = zero


def spread(sh, padded_ref, start, values):
    place = pl.ds(start + sh.cols, sh.chunk)
    spot = lax.broadcasted_iota(jnp.int32, values.shape, 0) % sh.cols
    padded_ref[0, place, :] = jnp.where(spot == 0, 0.0, pltpu.roll(values, 1, 0)).astype(jnp.bfloat16)
    padded_ref[1, place, :] = values.astype(jnp.bfloat16)
    padded_ref[2, place, :] = jnp.where(
        spot == sh.cols - 1, 0.0, pltpu.roll(values, sh.chunk - 1, 0)
    ).astype(jnp.bfloat16)


def convolve(sh, padded_ref, start, weight_ref, unit, backward):
    total = None
    for p in range(3):
        for q in range(3):
            row, col = (2 - p, 2 - q) if backward else (p, q)
            block = padded_ref[col, pl.ds(start + row * sh.cols, sh.chunk), :]
            tap = (3 * p + q) * sh.channels
            weight = weight_ref[unit, tap : tap + sh.channels, :]
            part = lax.dot_general(
                block,
                weight,
                (((1,), (1 if backward else 0,)), ((), ())),
                preferred_element_type=jnp.float32,
            )
            total = part if total is None else total + part
    return total


def forward_unit(sh, x_ref, out_ref, params, padded_ref, weight_ref, unit):
    factor, shift = params
    mean, inv_std = statistics(sh, x_ref)

    def activate(i):
        start = chunk_start(i, sh.chunk)
        normed = (x_ref[pl.ds(start, sh.chunk), :].astype(jnp.float32) - mean) * inv_std
        pre = normed * factor + shift
        spread(sh, padded_ref, start, pre * sigmoid(pre))

    def produce(i):
        start = chunk_start(i, sh.chunk)
        inputs = x_ref[pl.ds(start, sh.chunk), :].astype(jnp.float32)
        z = convolve(sh, padded_ref, start, weight_ref, unit, False)
        out_ref[pl.ds(start, sh.chunk), :] = (inputs + z).astype(jnp.bfloat16)

    over_chunks(sh.chunks, activate)
    over_chunks(sh.chunks, produce)


def backward_unit(sh, x_ref, up_ref, grad_ref, params, scratch, weight_ref, unit, keep_ref, send_ref, core):
    padded_ref, act_ref, slope_ref, pre_grad_ref, slab_ref = scratch
    factor, shift = params
    space = lax.axis_index("space")
    mean, inv_std = statistics(sh, x_ref)
    zero = jnp.zeros((8, sh.channels), jnp.float32)

    def activate(i):
        start = chunk_start(i, sh.chunk)
        rows = pl.ds(start, sh.chunk)
        spread(sh, padded_ref, start, up_ref[rows, :].astype(jnp.float32))
        pre = (x_ref[rows, :].astype(jnp.float32) - mean) * inv_std * factor + shift
        sigma = sigmoid(pre)
        act_ref[rows, :] = (pre * sigma).astype(jnp.bfloat16)
        slope_ref[rows, :] = sigma * (1.0 + pre * (1.0 - sigma))

    def differentiate(i, sums):
        start = chunk_start(i, sh.chunk)
        rows = pl.ds(start, sh.chunk)
        normed = (x_ref[rows, :].astype(jnp.float32) - mean) * inv_std
        pre_grad = convolve(sh, padded_ref, start, weight_ref, unit, True) * slope_ref[rows, :]
        pre_grad_ref[rows, :] = pre_grad
        return (sums[0] + fold_rows(pre_grad), sums[1] + fold_rows(pre_grad * normed))

    over_chunks(sh.chunks, activate)
    if sh.chunks == 1:
        sums = differentiate(0, (zero, zero))
    else:
        sums = lax.fori_loop(0, sh.chunks, differentiate, (zero, zero))
    sum_grad, sum_cross = column(sums[0]), column(sums[1])
    means = group_sums(stack_rows(factor * sum_grad, factor * sum_cross), sh.width) / sh.entries
    center, tilt = means[0:1], means[1:2]

    def finish(i):
        rows = pl.ds(chunk_start(i, sh.chunk), sh.chunk)
        normed = (x_ref[rows, :].astype(jnp.float32) - mean) * inv_std
        back = factor * pre_grad_ref[rows, :] - center - normed * tilt
        grad_ref[rows, :] = (up_ref[rows, :].astype(jnp.float32) + inv_std * back).astype(jnp.bfloat16)

    over_chunks(sh.chunks, finish)
    first_row = space * sh.slab
    first_tap = jnp.minimum(first_row // sh.channels, 9 - sh.taps)
    offset = pl.multiple_of(first_row - first_tap * sh.channels, 8)
    for t in range(sh.taps):
        tap = first_tap + t
        row, col = 2 - tap // 3, 2 - tap % 3
        place = pl.ds(t * sh.channels, sh.channels)

        def product(i):
            start = chunk_start(i, sh.chunk)
            block = padded_ref[col, pl.ds(pl.multiple_of(start + row * sh.cols, 16), sh.chunk), :]
            return lax.dot_general(
                act_ref[pl.ds(start, sh.chunk), :],
                block,
                (((0,), (0,)), ((), ())),
                preferred_element_type=jnp.float32,
            )

        if sh.chunks == 1:
            slab_ref[place, :] = product(0)
        else:
            slab_ref[place, :] = jnp.zeros((sh.channels, sh.channels), jnp.float32)

            def accumulate(i):
                slab_ref[place, :] += product(i)

            over_chunks(sh.chunks, accumulate)
    mine = slab_ref[pl.ds(offset, sh.slab), :]
    rows = grad_ref[pl.ds(pl.multiple_of(space * sh.own_rows, sh.own_rows), sh.own_rows), :]
    sums = stack_rows(sum_grad, sum_cross)

    def write(ref):
        ref[0 : sh.slab, :] = mine
        ref[sh.slab : sh.slab + sh.own_rows, :] = rows.astype(jnp.float32)
        ref[sh.slab + sh.own_rows : sh.pack, :] = sums

    @pl.when(core == unit)
    def _():
        write(keep_ref)

    @pl.when(core != unit)
    def _():
        write(send_ref)


def place_of():
    index = lax.axis_index("segment")
    return (index // PAIR, index % PAIR)


def unit_params(params_ref, unit):
    return (params_ref[2 * unit : 2 * unit + 1, :], params_ref[2 * unit + 1 : 2 * unit + 2, :])


def copies_kernel(block_ref, out_hbm, sems):
    copies = [
        pltpu.make_async_copy(block_ref, out_hbm.at[pl.ds(i, 1)], sems.at[i]) for i in range(out_hbm.shape[0])
    ]
    for copy in copies:
        copy.start()
    for copy in copies:
        copy.wait()


def prepare_kernel(
    times_ref,
    labels_ref,
    table_any,
    own_any,
    other_any,
    time_weight_ref,
    mod_weight_ref,
    mod_weight_other_ref,
    mod_bias_ref,
    mod_bias_other_ref,
    gain_ref,
    gain_other_ref,
    weights_ref,
    params_ref,
    embedded_ref,
    table_ref,
    sems,
):
    core = lax.axis_index("segment") % PAIR
    pairs = [(table_any.at[pl.ds(labels_ref[i] // 8, 1)], table_ref.at[pl.ds(i, 1)]) for i in range(PAIR)]
    pairs += [(own_any, weights_ref.at[core]), (other_any, weights_ref.at[1 - core])]
    copies = [pltpu.make_async_copy(a, b, sems.at[i]) for i, (a, b) in enumerate(pairs)]
    for copy in copies:
        copy.start()
    rows = 16
    spot = lax.broadcasted_iota(jnp.int32, (rows, 1), 0)
    time = jnp.where(spot % 2 == 0, times_ref[0], times_ref[1]).astype(jnp.float32)
    base = time_weight_ref.shape[0]
    half = base // 2
    lanes = lax.broadcasted_iota(jnp.int32, (rows, base), 1)
    power = jnp.where(lanes < half, lanes, lanes - half).astype(jnp.float32)
    angles = time * jnp.exp(-math.log(10000.0) * power / half)
    sinusoid = jnp.where(lanes < half, jnp.cos(angles), jnp.sin(angles)).astype(jnp.bfloat16)

    def label_row(image):
        block = table_ref[image].astype(jnp.float32)
        row = lax.broadcasted_iota(jnp.int32, block.shape, 0)
        return column(jnp.where(row == labels_ref[image] % 8, block, 0.0))

    timed = jnp.dot(sinusoid, time_weight_ref[...], preferred_element_type=jnp.float32)
    for copy in copies[:PAIR]:
        copy.wait()
    timed = timed + jnp.where(spot % 2 == 0, label_row(0), label_row(1))
    embedded = (timed * sigmoid(timed)).astype(jnp.bfloat16)
    embedded_ref[...] = embedded
    channels = gain_ref.shape[1]

    def factor_and_shift(weight, bias, gain):
        modulation = jnp.dot(embedded, weight[...], preferred_element_type=jnp.float32) + bias[...]
        modulation = jnp.where(core == 0, modulation[0:1], modulation[1:2])
        return (gain[...] * (1.0 + modulation[:, :channels]), modulation[:, channels:])

    own = factor_and_shift(mod_weight_ref, mod_bias_ref, gain_ref)
    other = factor_and_shift(mod_weight_other_ref, mod_bias_other_ref, gain_other_ref)
    row = lax.broadcasted_iota(jnp.int32, params_ref.shape, 0)
    factor = jnp.where(row // 2 == core, own[0], other[0])
    shift = jnp.where(row // 2 == core, own[1], other[1])
    params_ref[...] = jnp.where(row % 2 == 0, factor, shift)
    for copy in copies[PAIR:]:
        copy.wait()


def forward_kernel(sh, active_stage, x_ref, params_ref, weights, middle_ref, out_ref, padded_ref):
    stage, _ = place_of()

    @pl.when(stage == active_stage)
    def _():
        clear_edges(sh, padded_ref)
        forward_unit(sh, x_ref, middle_ref, unit_params(params_ref, 0), padded_ref, weights, 0)
        forward_unit(sh, middle_ref, out_ref, unit_params(params_ref, 1), padded_ref, weights, 1)


def backward_kernel(sh, active_stage, first, *refs):
    if first:
        x_ref, up_ref, params_ref, weights = refs[:4]
        refs = refs[4:]
    else:
        x_ref, middle_ref, up_ref, params_ref, weights, keep_in, send_in = refs[:7]
        refs = refs[7:]
    keep_ref, send_ref, grad_ref = refs[:3]
    padded_ref, act_ref, slope_ref, pre_grad_ref, slab_ref, between_ref = refs[3:9]
    if first:
        middle_ref = refs[9]
    stage, core = place_of()

    @pl.when(stage == active_stage)
    def _():
        clear_edges(sh, padded_ref)
        params = [unit_params(params_ref, unit) for unit in range(PAIR)]
        if first:
            forward_unit(sh, x_ref, middle_ref, params[0], padded_ref, weights, 0)
        scratch = (padded_ref, act_ref, slope_ref, pre_grad_ref, slab_ref)
        backward_unit(
            sh, middle_ref, up_ref, between_ref, params[1], scratch, weights, 1, keep_ref, send_ref, core
        )
        backward_unit(
            sh, x_ref, between_ref, grad_ref, params[0], scratch, weights, 0, keep_ref, send_ref, core
        )

    if not first:

        @pl.when(stage != active_stage)
        def _():
            keep_ref[...] = keep_in[...]
            send_ref[...] = send_in[...]


def finish_kernel(sh, keep_ref, other_ref, embedded_ref, gain_ref, grads_ref, conv_ref, mod_ref):
    core = lax.axis_index("segment") % PAIR
    conv_ref[...] = keep_ref[0 : sh.slab, :] + other_ref[0 : sh.slab, :]
    rows = slice(sh.slab, sh.slab + sh.own_rows)
    grads_ref[pl.ds(core, 1)] = keep_ref[rows, :].astype(jnp.bfloat16)[None]
    grads_ref[pl.ds(1 - core, 1)] = other_ref[rows, :].astype(jnp.bfloat16)[None]
    base = sh.slab + sh.own_rows

    def mod_rows(ref):
        return jnp.concatenate([gain_ref[...] * ref[base + 1 : base + 2, :], ref[base : base + 1, :]], axis=1)

    own, other = mod_rows(keep_ref), mod_rows(other_ref)
    spot = lax.broadcasted_iota(jnp.int32, (16, own.shape[1]), 0)
    values = jnp.where(spot % 2 == core, own, other)
    high = values.astype(jnp.bfloat16).astype(jnp.float32)
    rest = values - high
    middle = rest.astype(jnp.bfloat16).astype(jnp.float32)
    low = rest - middle
    part = spot // 2
    pieces = jnp.where(part == 0, high, jnp.where(part == 1, middle, jnp.where(part == 2, low, 0.0)))
    mod_ref[...] = lax.dot_general(
        embedded_ref[...],
        pieces.astype(jnp.bfloat16),
        (((0,), (0,)), ((), ())),
        preferred_element_type=jnp.float32,
    )


def shards(
    x_in,
    out_cotangent,
    timesteps,
    labels,
    time_weight,
    label_table,
    conv_weight,
    mod_weight,
    mod_bias,
    norm_gain,
):
    segments, spaces = lax.axis_size("segment"), lax.axis_size("space")
    stages = segments // PAIR
    stage, core = place_of()
    images, row_count, cols, channels = x_in.shape
    sh = Shape(row_count * spaces, cols, channels, spaces)
    f32, bf16 = jnp.float32, jnp.bfloat16

    def call(body, ins, outs, scratch=(), limit=sh.limit, cost=None):
        return pl.pallas_call(
            body,
            out_shape=outs,
            in_specs=ins,
            out_specs=[VMEM] * len(outs),
            scratch_shapes=list(scratch),
            compiler_params=pltpu.CompilerParams(vmem_limit_bytes=limit),
            cost_estimate=cost,
        )

    shape = jax.ShapeDtypeStruct
    swap = [(i, i ^ 1) for i in range(segments)]
    weight = conv_weight.reshape(9 * channels, channels)
    ends = jnp.where(stage == 0, x_in, out_cotangent)
    near = lax.dynamic_index_in_dim(ends, core, 0, keepdims=False).reshape(1, sh.own_rows, channels)
    copies = pl.pallas_call(
        copies_kernel,
        out_shape=shape((spaces, sh.own_rows, channels), bf16),
        in_specs=[VMEM],
        out_specs=ANY,
        scratch_shapes=[pltpu.SemaphoreType.DMA((spaces,))],
        cost_estimate=pl.CostEstimate(flops=2 << 34, bytes_accessed=1 << 20, transcendentals=0),
    )(near)
    image = lax.all_to_all(copies, "space", 0, 0).reshape(sh.pixels, channels)
    own = (mod_weight[0], mod_bias, norm_gain, weight)
    theirs = [lax.ppermute(value, "segment", swap) for value in own]
    table = label_table.reshape(-1, 8, label_table.shape[1])
    width = time_weight.shape[1]
    mods = [value for pair in zip(own[:3], theirs[:3]) for value in pair]
    weights, params, embedded = call(
        prepare_kernel,
        [SMEM, SMEM] + [ANY] * 3 + [VMEM] * 7,
        [shape((PAIR, 9 * channels, channels), bf16), shape((8, channels), f32), shape((16, width), bf16)],
        [pltpu.VMEM((PAIR, 8, width), bf16), pltpu.SemaphoreType.DMA((2 * PAIR,))],
        cost=pl.CostEstimate(flops=1 << 24, bytes_accessed=4 << 20, transcendentals=0),
    )(timesteps, labels, table, weight, theirs[3], time_weight, *mods)

    image_shape = shape((sh.pixels, channels), bf16)
    pack_shape = shape((sh.pack, channels), f32)
    common = [pltpu.VMEM((3, sh.padded, channels), bf16)]

    def hop(value, source, target):
        pairs = [(PAIR * source + k, PAIR * target + k) for k in range(PAIR)]
        return lax.ppermute(value, "segment", pairs)

    entering, middles = [image], []
    for active in range(stages - 1):
        middle, out = call(
            functools.partial(forward_kernel, sh, active),
            [VMEM] * 3,
            [image_shape, image_shape],
            common,
        )(entering[active], params, weights)
        middles.append(middle)
        entering.append(hop(out, active, active + 1))

    scratch = common + [
        pltpu.VMEM((sh.pixels, channels), bf16),
        pltpu.VMEM((sh.pixels, channels), f32),
        pltpu.VMEM((sh.pixels, channels), f32),
        pltpu.VMEM((sh.taps * channels, channels), f32),
        pltpu.VMEM((sh.pixels, channels), bf16),
    ]
    outs = [pack_shape, pack_shape, image_shape]
    keep, send, grad = call(
        functools.partial(backward_kernel, sh, stages - 1, True),
        [VMEM] * 4,
        outs,
        scratch + [pltpu.VMEM((sh.pixels, channels), bf16)],
    )(entering[stages - 1], image, params, weights)
    for active in range(stages - 2, -1, -1):
        upstream = hop(grad[0] if isinstance(grad, list) else grad, active + 1, active)
        last = active == 0
        keep, send, *grad = call(
            functools.partial(backward_kernel, sh, active, False),
            [VMEM] * 7,
            outs[:2] if last else outs,
            scratch[-1:] + scratch if last else scratch,
        )(entering[active], middles[active], upstream, params, weights, keep, send)
    other = lax.ppermute(send, "segment", swap)
    grads, conv_grad, mod_grad = call(
        functools.partial(finish_kernel, sh),
        [VMEM] * 4,
        [
            shape((images, sh.own_rows, channels), bf16),
            shape((sh.slab, channels), f32),
            shape((time_weight.shape[1], 2 * channels), f32),
        ],
    )(keep, other, embedded, norm_gain)
    return (grads.reshape(1, images, row_count, cols, channels), conv_grad[None], mod_grad[None])


def solution(mesh):
    placed = (
        P(None, "space", None, None),
        P(None, "space", None, None),
        P(),
        P(),
        P(),
        P(),
        P("segment", None, None, None, None),
        P("segment", None, None),
        P("segment", None),
        P("segment", None),
    )
    return jax.shard_map(
        shards,
        mesh=mesh,
        in_specs=placed,
        out_specs=(
            P("segment", None, "space", None, None),
            P("segment", "space", None),
            P("segment", None, None),
        ),
        check_vma=False,
    )
```

profile of v0, /device:TPU:0, one launch (start us, length us, event | category | flops | bytes accessed | tf_op | source)
XLA Modules:
  0.0 44.2 jit_solution(4126659723085228836)
XLA Ops:
  0.6 0.5 %collective-permute-start.1 = (bf16[512,512]{1,0:T(8,128)(2,1)}, bf16[512,512]{1,0:T(8,128)(2,1)S(1)}, u32[]{:S(2)}, u32[]{:S(2)}) collective-permute-start(bf16[512,512]{1,0:T(8,128)(2,1)} %bitcast.14), channel_id=1, source_target_pairs={{0,8},{8,0},{16,24},{24,16},{1,9},{9,1},{17,25},{25,17},{2,10},{10... | collective-permute-start | bytes 1572872 | tf_op jit(solution)/shard_map/ppermute | solution.py:435
  1.1 0.1 collective-permute-start
  1.2 1.3 %dynamic-slice_select_fusion = bf16[1,2,16,256]{3,2,1,0:T(8,128)(2,1)} fusion(bf16[2,2,16,256]{3,2,1,0:T(8,128)(2,1)} %param.11, s32[]{:T(128)S(6)} %select_n.27, bf16[2,2,16,256]{3,2,1,0:T(8,128)(2,1)} %param.10, pred[]{:T(512)S(6)} %eq.5), kind=kLoop, calls=%fused_computation | loop fusion | flops 8192 | bytes 49157 | tf_op jit(solution)/shard_map/jit(_where)/select_n | solution.py:423
  2.6 1.5 %shard_map.121 = bf16[8,32,256]{2,1,0:T(8,128)(2,1)} custom-call(bf16[1,32,256]{2,1,0:T(8,128)(2,1)} %bitcast.16), custom_call_target="tpu_custom_call" | custom-call | flops 34359738368 | bytes 1048576 | tf_op jit(solution)/shard_map/pallas_call | solution.py:425
  4.1 7.2 %all-to-all-start = ((bf16[8,32,256]{2,1,0:T(8,128)(2,1)}), bf16[8,32,256]{2,1,0:T(8,128)(2,1)S(1)}, u32[]{:S(2)}, u32[]{:S(2)}) async-start(bf16[8,32,256]{2,1,0:T(8,128)(2,1)} %shard_map.121), calls=%async_computation | async-start | bytes 262144 | tf_op jit(solution)/shard_map/all_to_all | solution.py:433
  11.4 0.1 collective-permute-start.2
  11.5 0.5 %collective-permute-start.3 = (f32[1,256]{1,0:T(1,128)S(1)}, f32[1,256]{1,0:T(1,128)S(1)}, u32[]{:S(2)}, u32[]{:S(2)}) collective-permute-start(f32[1,256]{1,0:T(1,128)S(1)} %copy-done.8), channel_id=1, source_target_pairs={{0,8},{8,0},{16,24},{24,16},{1,9},{9,1},{17,25},{25,17},{2,10},{10... | collective-permute-start | bytes 3080 | tf_op jit(solution)/shard_map/ppermute | solution.py:435
  12.0 0.8 %collective-permute-done.3.gain_other_ref = f32[1,256]{1,0:T(1,128)S(1)} collective-permute-done((f32[1,256]{1,0:T(1,128)S(1)}, f32[1,256]{1,0:T(1,128)S(1)}, u32[]{:S(2)}, u32[]{:S(2)}) %collective-permute-start.3) | collective-permute-done | bytes 1056 | tf_op jit(solution)/shard_map/ppermute | solution.py:435
  12.8 0.8 %copy-done.5 = bf16[512,512]{1,0:T(8,128)(2,1)} copy-done((bf16[512,512]{1,0:T(8,128)(2,1)}, bf16[512,512]{1,0:T(8,128)(2,1)S(1)}, u32[]{:S(2)}) %copy-start.5) | copy-done | bytes 524312
  13.6 1.0 %copy-done.1 = bf16[2304,256]{1,0:T(8,128)(2,1)} copy-done((bf16[2304,256]{1,0:T(8,128)(2,1)}, bf16[2304,256]{1,0:T(8,128)(2,1)S(1)}, u32[]{:S(2)}) %copy-start.1) | copy-done | bytes 1179672
  14.6 1.3 %copy-done = bf16[1,3,3,256,256]{4,3,2,1,0:T(8,128)(2,1)S(1)} copy-done((bf16[1,3,3,256,256]{4,3,2,1,0:T(8,128)(2,1)S(1)}, bf16[1,3,3,256,256]{4,3,2,1,0:T(8,128)(2,1)}, u32[]{:S(2)}) %copy-start) | copy-done | bytes 1179672
  15.9 1.3 %copy-done.2 = bf16[2304,256]{1,0:T(8,128)(2,1)S(1)} copy-done((bf16[2304,256]{1,0:T(8,128)(2,1)S(1)}, bf16[2304,256]{1,0:T(8,128)(2,1)}, u32[]{:S(2)}) %copy-start.2) | copy-done | bytes 1179672
  17.2 1.0 %copy-done.4 = bf16[1,512,512]{2,1,0:T(8,128)(2,1)S(1)} copy-done((bf16[1,512,512]{2,1,0:T(8,128)(2,1)S(1)}, bf16[1,512,512]{2,1,0:T(8,128)(2,1)}, u32[]{:S(2)}) %copy-start.4) | copy-done | bytes 524312
  18.2 1.0 %copy-done.6 = bf16[512,512]{1,0:T(8,128)(2,1)S(1)} copy-done((bf16[512,512]{1,0:T(8,128)(2,1)S(1)}, bf16[512,512]{1,0:T(8,128)(2,1)}, u32[]{:S(2)}) %copy-start.6) | copy-done | bytes 524312
  19.3 0.9 %copy-done.7 = bf16[128,512]{1,0:T(8,128)(2,1)S(1)} copy-done((bf16[128,512]{1,0:T(8,128)(2,1)S(1)}, bf16[128,512]{1,0:T(8,128)(2,1)}, u32[]{:S(2)}) %copy-start.7) | copy-done | bytes 131096
  20.2 1.5 %shard_map.122 = (bf16[2,2304,256]{2,1,0:T(8,128)(2,1)S(1)}, f32[8,256]{1,0:T(8,128)S(1)}, bf16[16,512]{1,0:T(8,128)(2,1)S(1)}) custom-call(s32[2]{0:T(128)S(1)} %copy-done.10, s32[2]{0:T(128)S(1)} %copy-done.11, bf16[125,8,512]{2,1,0:T(8,128)(2,1)S(1)} %bitcast.13, bf16[2304,256]{1,0:T(8,128)(2,1)S(1)} %bitcast.12, bf16[2304,256]{1,0:T(8,128)(2,1)S(1)} %copy-done.2, ...), custom_call_target="tpu_custom_call" | custom-call | flops 16777216 | bytes 4194304 | tf_op jit(solution)/shard_map/pallas_call | solution.py:439
  21.7 2.0 %shard_map.123 = (bf16[256,256]{1,0:T(8,128)(2,1)S(1)}, bf16[256,256]{1,0:T(8,128)(2,1)S(1)}) custom-call(bf16[256,256]{1,0:T(8,128)(2,1)S(1)} %bitcast.8, f32[8,256]{1,0:T(8,128)S(1)} %get-tuple-element.16.params_ref.refs_2_.refs_3_, bf16[2,2304,256]{2,1,0:T(8,128)(2,1)S(1)} %get-tuple-element.17.weights.refs_3_.refs_4_), custom_call_target="tpu_custom_call" | custom-call | tf_op jit(solution)/shard_map/pallas_call | solution.py:457
  23.8 1.4 %collective-permute-start.4 = (bf16[256,256]{1,0:T(8,128)(2,1)S(1)}, bf16[256,256]{1,0:T(8,128)(2,1)S(1)}, u32[]{:S(2)}, u32[]{:S(2)}) collective-permute-start(bf16[256,256]{1,0:T(8,128)(2,1)S(1)} %get-tuple-element.19), channel_id=1, source_target_pairs={{0,16},{8,24},{1,17},{9,25},{2,18},{10,26},{3,19},{11,27},{4,20},{... | collective-permute-start | bytes 393224 | tf_op jit(solution)/shard_map/ppermute | solution.py:453
  25.2 3.4 %collective-permute-done.4.refs_0_ = bf16[256,256]{1,0:T(8,128)(2,1)S(1)} collective-permute-done((bf16[256,256]{1,0:T(8,128)(2,1)S(1)}, bf16[256,256]{1,0:T(8,128)(2,1)S(1)}, u32[]{:S(2)}, u32[]{:S(2)}) %collective-permute-start.4) | collective-permute-done | bytes 131104 | tf_op jit(solution)/shard_map/ppermute | solution.py:453
  28.6 1.3 %collective-permute-start.5 = (bf16[256,256]{1,0:T(8,128)(2,1)S(1)}, bf16[256,256]{1,0:T(8,128)(2,1)S(1)}, u32[]{:S(2)}, u32[]{:S(2)}) collective-permute-start(bf16[256,256]{1,0:T(8,128)(2,1)S(1)} %get-tuple-element.20), channel_id=1, source_target_pairs={{16,0},{24,8},{17,1},{25,9},{18,2},{26,10},{19,3},{27,11},{20,4},{... | collective-permute-start | bytes 393224 | tf_op jit(solution)/shard_map/ppermute | solution.py:453
  29.9 9.0 %collective-permute-done.5.refs_2_ = bf16[256,256]{1,0:T(8,128)(2,1)S(1)} collective-permute-done((bf16[256,256]{1,0:T(8,128)(2,1)S(1)}, bf16[256,256]{1,0:T(8,128)(2,1)S(1)}, u32[]{:S(2)}, u32[]{:S(2)}) %collective-permute-start.5) | collective-permute-done | bytes 131104 | tf_op jit(solution)/shard_map/ppermute | solution.py:453
  38.9 2.3 %shard_map.125 = (f32[328,256]{1,0:T(8,128)S(1)}, f32[328,256]{1,0:T(8,128)S(1)}) custom-call(bf16[256,256]{1,0:T(8,128)(2,1)S(1)} %bitcast.10, bf16[256,256]{1,0:T(8,128)(2,1)S(1)} %get-tuple-element.18.refs_1_, bf16[256,256]{1,0:T(8,128)(2,1)S(1)} %collective-permute-done.5.refs_2_, f32[8,256]{1,0:T(8,128)S(1)} %get-tuple-element.16.params_ref.refs_2_.refs_3_, ...), custom_call_target="tpu_custom_call" | custom-call | tf_op jit(solution)/shard_map/pallas_call | solution.py:483
  41.2 1.6 %collective-permute-done.6.other_ref = f32[328,256]{1,0:T(8,128)S(1)} collective-permute-done((f32[328,256]{1,0:T(8,128)S(1)}, f32[328,256]{1,0:T(8,128)S(1)}, u32[]{:S(2)}, u32[]{:S(2)}) %collective-permute-start.6) | collective-permute-done | bytes 335904 | tf_op jit(solution)/shard_map/ppermute | solution.py:489
  42.9 1.4 %shard_map.126 = (bf16[2,32,256]{2,1,0:T(8,128)(2,1)}, f32[288,256]{1,0:T(8,128)}, f32[512,512]{1,0:T(8,128)}) custom-call(f32[328,256]{1,0:T(8,128)S(1)} %get-tuple-element.23.keep_ref, f32[328,256]{1,0:T(8,128)S(1)} %collective-permute-done.6.other_ref, bf16[16,512]{1,0:T(8,128)(2,1)S(1)} %get-tuple-element.25.embedded_ref, f32[1,256]{1,0:T(1,128)S(1)} %copy-done.8), custom_call_target="tpu_custom_call" | custom-call | tf_op jit(solution)/shard_map/pallas_call | solution.py:490
  (23 shorter events, 0.1 us)
Async XLA Ops:
  0.6 12.1 %collective-permute-start.1 = (bf16[512,512]{1,0:T(8,128)(2,1)}, bf16[512,512]{1,0:T(8,128)(2,1)S(1)}, u32[]{:S(2)}, u32[]{:S(2)}) collective-permute-start(bf16[512,512]{1,0:T(8,128)(2,1)} %bitcast.14), channel_id=1, source_target_pairs={{0,8},{8,0},{16,24},{24,16},{1,9},{9,1},{17,25},{25,17},{2,10},{10... | collective-permute-start | bytes 1572872 | tf_op jit(solution)/shard_map/ppermute | solution.py:435
  1.1 12.4 %collective-permute-start = (bf16[2304,256]{1,0:T(8,128)(2,1)}, bf16[2304,256]{1,0:T(8,128)(2,1)S(1)}, u32[]{:S(2)}, u32[]{:S(2)}) collective-permute-start(bf16[2304,256]{1,0:T(8,128)(2,1)} %bitcast.11), channel_id=1, source_target_pairs={{0,8},{8,0},{16,24},{24,16},{1,9},{9,1},{17,25},{25,17},{2,10},{10... | collective-permute-start | bytes 3538952 | tf_op jit(solution)/shard_map/ppermute | solution.py:435
  2.6 8.8 %copy-start.9 = (f32[1,512]{1,0:T(1,128)S(1)}, f32[1,512]{1,0:T(1,128)}, u32[]{:S(2)}) copy-start(f32[1,512]{1,0:T(1,128)} %mod_bias_ref.1) | copy-start | bytes 6148
  2.6 8.9 %copy-start.8 = (f32[1,256]{1,0:T(1,128)S(1)}, f32[1,256]{1,0:T(1,128)}, u32[]{:S(2)}) copy-start(f32[1,256]{1,0:T(1,128)} %gain_ref.3) | copy-start | bytes 3076
  2.6 12.0 %copy-start.3 = (bf16[1000,512]{1,0:T(8,128)(2,1)S(1)}, bf16[1000,512]{1,0:T(8,128)(2,1)}, u32[]{:S(2)}) copy-start(bf16[1000,512]{1,0:T(8,128)(2,1)} %param.15) | copy-start | bytes 3072004
  2.6 12.0 %copy-start.10 = (s32[2]{0:T(128)S(1)}, s32[2]{0:T(128)}, u32[]{:S(2)}) copy-start(s32[2]{0:T(128)} %times_ref.1) | copy-start | bytes 28
  2.6 12.0 %copy-start.11 = (s32[2]{0:T(128)S(1)}, s32[2]{0:T(128)}, u32[]{:S(2)}) copy-start(s32[2]{0:T(128)} %labels_ref.1) | copy-start | bytes 28
  4.1 17.6 %all-to-all-start = ((bf16[8,32,256]{2,1,0:T(8,128)(2,1)}), bf16[8,32,256]{2,1,0:T(8,128)(2,1)S(1)}, u32[]{:S(2)}, u32[]{:S(2)}) async-start(bf16[8,32,256]{2,1,0:T(8,128)(2,1)} %shard_map.121), calls=%async_computation | async-start | bytes 262144 | tf_op jit(solution)/shard_map/all_to_all | solution.py:433
  11.4 1.4 %collective-permute-start.2 = (f32[1,512]{1,0:T(1,128)S(1)}, f32[1,512]{1,0:T(1,128)S(1)}, u32[]{:S(2)}, u32[]{:S(2)}) collective-permute-start(f32[1,512]{1,0:T(1,128)S(1)} %copy-done.9), channel_id=1, source_target_pairs={{0,8},{8,0},{16,24},{24,16},{1,9},{9,1},{17,25},{25,17},{2,10},{10... | collective-permute-start | bytes 6152 | tf_op jit(solution)/shard_map/ppermute | solution.py:435
  11.5 1.3 %collective-permute-start.3 = (f32[1,256]{1,0:T(1,128)S(1)}, f32[1,256]{1,0:T(1,128)S(1)}, u32[]{:S(2)}, u32[]{:S(2)}) collective-permute-start(f32[1,256]{1,0:T(1,128)S(1)} %copy-done.8), channel_id=1, source_target_pairs={{0,8},{8,0},{16,24},{24,16},{1,9},{9,1},{17,25},{25,17},{2,10},{10... | collective-permute-start | bytes 3080 | tf_op jit(solution)/shard_map/ppermute | solution.py:435
  12.8 0.8 %copy-start.5 = (bf16[512,512]{1,0:T(8,128)(2,1)}, bf16[512,512]{1,0:T(8,128)(2,1)S(1)}, u32[]{:S(2)}) copy-start(bf16[512,512]{1,0:T(8,128)(2,1)S(1)} %collective-permute-done.1.mod_weight_other_ref) | copy-start | bytes 1572868
  13.6 1.0 %copy-start.1 = (bf16[2304,256]{1,0:T(8,128)(2,1)}, bf16[2304,256]{1,0:T(8,128)(2,1)S(1)}, u32[]{:S(2)}) copy-start(bf16[2304,256]{1,0:T(8,128)(2,1)S(1)} %collective-permute-done.other_any) | copy-start | bytes 3538948
  14.6 1.3 %copy-start = (bf16[1,3,3,256,256]{4,3,2,1,0:T(8,128)(2,1)S(1)}, bf16[1,3,3,256,256]{4,3,2,1,0:T(8,128)(2,1)}, u32[]{:S(2)}) copy-start(bf16[1,3,3,256,256]{4,3,2,1,0:T(8,128)(2,1)} %param.16) | copy-start | bytes 3538948
  15.9 1.3 %copy-start.2 = (bf16[2304,256]{1,0:T(8,128)(2,1)S(1)}, bf16[2304,256]{1,0:T(8,128)(2,1)}, u32[]{:S(2)}) copy-start(bf16[2304,256]{1,0:T(8,128)(2,1)} %copy-done.1) | copy-start | bytes 3538948
  17.2 1.0 %copy-start.4 = (bf16[1,512,512]{2,1,0:T(8,128)(2,1)S(1)}, bf16[1,512,512]{2,1,0:T(8,128)(2,1)}, u32[]{:S(2)}) copy-start(bf16[1,512,512]{2,1,0:T(8,128)(2,1)} %param.17) | copy-start | bytes 1572868
  18.2 1.0 %copy-start.6 = (bf16[512,512]{1,0:T(8,128)(2,1)S(1)}, bf16[512,512]{1,0:T(8,128)(2,1)}, u32[]{:S(2)}) copy-start(bf16[512,512]{1,0:T(8,128)(2,1)} %copy-done.5) | copy-start | bytes 1572868
  19.3 0.9 %copy-start.7 = (bf16[128,512]{1,0:T(8,128)(2,1)S(1)}, bf16[128,512]{1,0:T(8,128)(2,1)}, u32[]{:S(2)}) copy-start(bf16[128,512]{1,0:T(8,128)(2,1)} %time_weight_ref.1) | copy-start | bytes 393220
  23.8 4.8 %collective-permute-start.4 = (bf16[256,256]{1,0:T(8,128)(2,1)S(1)}, bf16[256,256]{1,0:T(8,128)(2,1)S(1)}, u32[]{:S(2)}, u32[]{:S(2)}) collective-permute-start(bf16[256,256]{1,0:T(8,128)(2,1)S(1)} %get-tuple-element.19), channel_id=1, source_target_pairs={{0,16},{8,24},{1,17},{9,25},{2,18},{10,26},{3,19},{11,27},{4,20},{... | collective-permute-start | bytes 393224 | tf_op jit(solution)/shard_map/ppermute | solution.py:453
  28.6 10.3 %collective-permute-start.5 = (bf16[256,256]{1,0:T(8,128)(2,1)S(1)}, bf16[256,256]{1,0:T(8,128)(2,1)S(1)}, u32[]{:S(2)}, u32[]{:S(2)}) collective-permute-start(bf16[256,256]{1,0:T(8,128)(2,1)S(1)} %get-tuple-element.20), channel_id=1, source_target_pairs={{16,0},{24,8},{17,1},{25,9},{18,2},{26,10},{19,3},{27,11},{20,4},{... | collective-permute-start | bytes 393224 | tf_op jit(solution)/shard_map/ppermute | solution.py:453
  41.1 1.7 %collective-permute-start.6 = (f32[328,256]{1,0:T(8,128)S(1)}, f32[328,256]{1,0:T(8,128)S(1)}, u32[]{:S(2)}, u32[]{:S(2)}) collective-permute-start(f32[328,256]{1,0:T(8,128)S(1)} %get-tuple-element.24), channel_id=1, source_target_pairs={{0,8},{8,0},{16,24},{24,16},{1,9},{9,1},{17,25},{25,17},{2,10},{10... | collective-permute-start | bytes 1007624 | tf_op jit(solution)/shard_map/ppermute | solution.py:489
where the time goes:
time: 44.8 us; the launch traced here: 44.2 us
  waiting for transfers between devices  14.8 us (33%)
  starting transfers between devices  11.2 us (25%)
  Pallas kernels  8.73 us (19%)
  local copies, waits for them, and re-layouts  7.38 us (16%)
  other arithmetic  1.34 us (3%)
  between operations  0.75 us (2%)
    ppermute x2, waiting for transfers between devices, hop(): return lax.ppermute(value, 'segment', pairs)  12.4 us
    unnamed x24, local copies, waits for them, and re-layouts  7.38 us
    all_to_all x1, starting transfers between devices, shards(): image = lax.all_to_all(copies, 'space', 0, 0).reshape(sh.pixels, channels)  7.24 us
    ppermute x2, starting transfers between devices, hop(): return lax.ppermute(value, 'segment', pairs)  2.69 us
    pallas_call x1, Pallas kernels, shards(): call(functools.partial(backward_kernel, sh, active, False), [VMEM] * 7, o...  2.26 us
    pallas_call x1, Pallas kernels, shards(): call(functools.partial(forward_kernel, sh, active), [VMEM] * 3, [image_sh...  2.04 us
    ppermute x1, waiting for transfers between devices, shards(): other = lax.ppermute(send, 'segment', swap)  1.63 us
    pallas_call x1, Pallas kernels, shards(): call(prepare_kernel, [SMEM, SMEM] + [ANY] * 3 + [VMEM] * 7, [shape((PAIR,...  1.54 us
  transfers between devices with their start and end apart: 8, of which 4 were waited for; matrix products, arithmetic and copies ran while one was open for 3% of the time, Pallas kernels for 7%

commit v1 on v0

--- a/solution.py
+++ b/solution.py
@@ -11,6 +11,8 @@
 GROUPS = 32
 EPSILON = 1e-05
 PAIR = 2
+PREPARE_LIMIT = 60 << 20
+CHAIN_LIMIT = 48 << 20
 VMEM = pl.BlockSpec(memory_space=pltpu.VMEM)
 SMEM = pl.BlockSpec(memory_space=pltpu.SMEM)
 ANY = pl.BlockSpec(memory_space=pl.ANY)
@@ -241,80 +243,99 @@
     return (params_ref[2 * unit : 2 * unit + 1, :], params_ref[2 * unit + 1 : 2 * unit + 2, :])
 
 
-def copies_kernel(block_ref, out_hbm, sems):
-    copies = [
-        pltpu.make_async_copy(block_ref, out_hbm.at[pl.ds(i, 1)], sems.at[i]) for i in range(out_hbm.shape[0])
-    ]
-    for copy in copies:
-        copy.start()
-    for copy in copies:
-        copy.wait()
-
-
-def prepare_kernel(
-    times_ref,
-    labels_ref,
-    table_any,
-    own_any,
-    other_any,
-    time_weight_ref,
-    mod_weight_ref,
-    mod_weight_other_ref,
-    mod_bias_ref,
-    mod_bias_other_ref,
-    gain_ref,
-    gain_other_ref,
-    weights_ref,
-    params_ref,
-    embedded_ref,
-    table_ref,
-    sems,
-):
-    core = lax.axis_index("segment") % PAIR
-    pairs = [(table_any.at[pl.ds(labels_ref[i] // 8, 1)], table_ref.at[pl.ds(i, 1)]) for i in range(PAIR)]
-    pairs += [(own_any, weights_ref.at[core]), (other_any, weights_ref.at[1 - core])]
+def sinusoid_of(time, base):
+    half = base // 2
+    lanes = lax.broadcasted_iota(jnp.int32, (time.shape[0], base), 1)
+    power = jnp.where(lanes < half, lanes, lanes - half).astype(jnp.float32)
+    angle = time * jnp.exp(-math.log(10000.0) * power / half)
+    turns = jnp.floor(angle * (2.0 / math.pi) + 0.5)
+    rest = ((angle - turns * 1.5703125) - turns * 4.83751296997e-4) - turns * 7.54978995489e-8
+    square = rest * rest
+    sine = rest + rest * square * (
+        -1.6666654611e-1 + square * (8.3321608736e-3 - square * 1.9515295891e-4)
+    )
+    cosine = 1.0 - 0.5 * square + square * square * (
+        4.166664568298827e-2 + square * (-1.388731625493765e-3 + square * 2.443315711809948e-5)
+    )
+    quarter = turns.astype(jnp.int32) + jnp.where(lanes < half, 1, 0)
+    value = jnp.where(quarter % 2 == 1, cosine, sine)
+    return jnp.where((quarter // 2) % 2 == 1, -value, value).astype(jnp.bfloat16)
+
+
+def start_all(pairs, sems):
     copies = [pltpu.make_async_copy(a, b, sems.at[i]) for i, (a, b) in enumerate(pairs)]
     for copy in copies:
         copy.start()
-    rows = 16
-    spot = lax.broadcasted_iota(jnp.int32, (rows, 1), 0)
+    return copies
+
+
+def embed_kernel(times_ref, labels_ref, table_hbm, time_weight_hbm, embedded_ref, table_ref, time_weight_ref, sems):
+    pairs = [(time_weight_hbm, time_weight_ref)]
+    pairs += [(table_hbm.at[pl.ds(labels_ref[i] // 8, 1)], table_ref.at[pl.ds(i, 1)]) for i in range(PAIR)]
+    copies = start_all(pairs, sems)
+    spot = lax.broadcasted_iota(jnp.int32, (16, 1), 0)
     time = jnp.where(spot % 2 == 0, times_ref[0], times_ref[1]).astype(jnp.float32)
-    base = time_weight_ref.shape[0]
-    half = base // 2
-    lanes = lax.broadcasted_iota(jnp.int32, (rows, base), 1)
-    power = jnp.where(lanes < half, lanes, lanes - half).astype(jnp.float32)
-    angles = time * jnp.exp(-math.log(10000.0) * power / half)
-    sinusoid = jnp.where(lanes < half, jnp.cos(angles), jnp.sin(angles)).astype(jnp.bfloat16)
+    sinusoid = sinusoid_of(time, time_weight_ref.shape[0])
 
     def label_row(image):
         block = table_ref[image].astype(jnp.float32)
         row = lax.broadcasted_iota(jnp.int32, block.shape, 0)
         return column(jnp.where(row == labels_ref[image] % 8, block, 0.0))
 
+    for copy in copies:
+        copy.wait()
     timed = jnp.dot(sinusoid, time_weight_ref[...], preferred_element_type=jnp.float32)
+    timed = timed + jnp.where(spot % 2 == 0, label_row(0), label_row(1))
+    embedded_ref[...] = (timed * sigmoid(timed)).astype(jnp.bfloat16)
+
+
+def modulate_kernel(embedded_hbm, mod_weight_hbm, bias_hbm, gain_hbm, keep_ref, send_ref, *scratch):
+    embedded_ref, mod_weight_ref, bias_ref, gain_ref, sems = scratch
+    core = lax.axis_index("segment") % PAIR
+    copies = start_all(zip((embedded_hbm, mod_weight_hbm, bias_hbm, gain_hbm), scratch[:4]), sems)
+    for copy in copies:
+        copy.wait()
+    modulation = jnp.dot(embedded_ref[...], mod_weight_ref[...], preferred_element_type=jnp.float32) + bias_ref[...]
+    channels = gain_ref.shape[1]
+    factor = gain_ref[...] * (1.0 + modulation[:, :channels])
+    shift = modulation[:, channels:]
+    first = stack_rows(factor[0:1], shift[0:1])
+    second = stack_rows(factor[1:2], shift[1:2])
+    keep_ref[...] = jnp.where(core == 0, first, second)
+    send_ref[...] = jnp.where(core == 0, second, first)
+
+
+def layout_kernel(own_any, other_any, mod_keep_any, mod_other_any, weights_ref, params_ref, mods_ref, sems):
+    core = lax.axis_index("segment") % PAIR
+    pairs = [(mod_keep_any, mods_ref.at[core]), (mod_other_any, mods_ref.at[1 - core])]
+    pairs += [(own_any, weights_ref.at[core]), (other_any, weights_ref.at[1 - core])]
+    copies = start_all(pairs, sems)
     for copy in copies[:PAIR]:
         copy.wait()
-    timed = timed + jnp.where(spot % 2 == 0, label_row(0), label_row(1))
-    embedded = (timed * sigmoid(timed)).astype(jnp.bfloat16)
-    embedded_ref[...] = embedded
-    channels = gain_ref.shape[1]
-
-    def factor_and_shift(weight, bias, gain):
-        modulation = jnp.dot(embedded, weight[...], preferred_element_type=jnp.float32) + bias[...]
-        modulation = jnp.where(core == 0, modulation[0:1], modulation[1:2])
-        return (gain[...] * (1.0 + modulation[:, :channels]), modulation[:, channels:])
-
-    own = factor_and_shift(mod_weight_ref, mod_bias_ref, gain_ref)
-    other = factor_and_shift(mod_weight_other_ref, mod_bias_other_ref, gain_other_ref)
-    row = lax.broadcasted_iota(jnp.int32, params_ref.shape, 0)
-    factor = jnp.where(row // 2 == core, own[0], other[0])
-    shift = jnp.where(row // 2 == core, own[1], other[1])
-    params_ref[...] = jnp.where(row % 2 == 0, factor, shift)
+    params_ref[0:2, :] = mods_ref[0, 0:2, :]
+    params_ref[2:4, :] = mods_ref[1, 0:2, :]
+    params_ref[4:8, :] = jnp.zeros((4, params_ref.shape[1]), jnp.float32)
     for copy in copies[PAIR:]:
         copy.wait()
 
 
-def forward_kernel(sh, active_stage, x_ref, params_ref, weights, middle_ref, out_ref, padded_ref):
+def assemble(sh, blocks_ref, order, image_ref):
+    space = lax.axis_index("space")
+    for k, bits in enumerate(order):
+        start = pl.multiple_of((space ^ bits) * sh.own_rows, sh.own_rows)
+        image_ref[pl.ds(start, sh.own_rows), :] = blocks_ref[k]
+
+
+def forward_kernel(sh, active_stage, orders, *refs):
+    if orders:
+        near_ref, far_ref, params_ref, weights, x_ref = refs[:5]
+        assemble(sh, near_ref, orders[0], x_ref)
+        assemble(sh, far_ref, orders[1], x_ref)
+        refs = refs[5:]
+    else:
+        x_ref, params_ref, weights = refs[:3]
+        refs = refs[3:]
+    middle_ref, out_ref, padded_ref = refs
     stage, _ = place_of()
 
     @pl.when(stage == active_stage)
@@ -329,7 +350,7 @@
         x_ref, up_ref, params_ref, weights = refs[:4]
         refs = refs[4:]
     else:
-        x_ref, middle_ref, up_ref, params_ref, weights, keep_in, send_in = refs[:7]
+        x_ref, middle_ref, up_ref, params_ref, weights = refs[:5]
         refs = refs[7:]
     keep_ref, send_ref, grad_ref = refs[:3]
     padded_ref, act_ref, slope_ref, pre_grad_ref, slab_ref, between_ref = refs[3:9]
@@ -350,13 +371,6 @@
         backward_unit(
             sh, x_ref, between_ref, grad_ref, params[0], scratch, weights, 0, keep_ref, send_ref, core
         )
-
-    if not first:
-
-        @pl.when(stage != active_stage)
-        def _():
-            keep_ref[...] = keep_in[...]
-            send_ref[...] = send_in[...]
 
 
 def finish_kernel(sh, keep_ref, other_ref, embedded_ref, gain_ref, grads_ref, conv_ref, mod_ref):
@@ -406,13 +420,14 @@
     sh = Shape(row_count * spaces, cols, channels, spaces)
     f32, bf16 = jnp.float32, jnp.bfloat16
 
-    def call(body, ins, outs, scratch=(), limit=sh.limit, cost=None):
+    def call(body, ins, outs, scratch=(), limit=CHAIN_LIMIT, cost=None, aliases={}):
         return pl.pallas_call(
             body,
             out_shape=outs,
             in_specs=ins,
             out_specs=[VMEM] * len(outs),
             scratch_shapes=list(scratch),
+            input_output_aliases=aliases,
             compiler_params=pltpu.CompilerParams(vmem_limit_bytes=limit),
             cost_estimate=cost,
         )
@@ -420,29 +435,56 @@
     shape = jax.ShapeDtypeStruct
     swap = [(i, i ^ 1) for i in range(segments)]
     weight = conv_weight.reshape(9 * channels, channels)
+    other_weight = lax.ppermute(weight, "segment", swap)
     ends = jnp.where(stage == 0, x_in, out_cotangent)
     near = lax.dynamic_index_in_dim(ends, core, 0, keepdims=False).reshape(1, sh.own_rows, channels)
-    copies = pl.pallas_call(
-        copies_kernel,
-        out_shape=shape((spaces, sh.own_rows, channels), bf16),
-        in_specs=[VMEM],
-        out_specs=ANY,
-        scratch_shapes=[pltpu.SemaphoreType.DMA((spaces,))],
-        cost_estimate=pl.CostEstimate(flops=2 << 34, bytes_accessed=1 << 20, transcendentals=0),
-    )(near)
-    image = lax.all_to_all(copies, "space", 0, 0).reshape(sh.pixels, channels)
-    own = (mod_weight[0], mod_bias, norm_gain, weight)
-    theirs = [lax.ppermute(value, "segment", swap) for value in own]
     table = label_table.reshape(-1, 8, label_table.shape[1])
     width = time_weight.shape[1]
-    mods = [value for pair in zip(own[:3], theirs[:3]) for value in pair]
-    weights, params, embedded = call(
-        prepare_kernel,
-        [SMEM, SMEM] + [ANY] * 3 + [VMEM] * 7,
-        [shape((PAIR, 9 * channels, channels), bf16), shape((8, channels), f32), shape((16, width), bf16)],
-        [pltpu.VMEM((PAIR, 8, width), bf16), pltpu.SemaphoreType.DMA((2 * PAIR,))],
-        cost=pl.CostEstimate(flops=1 << 24, bytes_accessed=4 << 20, transcendentals=0),
-    )(timesteps, labels, table, weight, theirs[3], time_weight, *mods)
+    some = pl.CostEstimate(flops=1 << 20, bytes_accessed=4 << 20, transcendentals=0)
+    order, bit = [0], spaces // 2
+    waiting = []
+    while True:
+        far = lax.ppermute(near, "space", [(i, i ^ bit) for i in range(spaces)])
+        if not waiting:
+            (embedded,) = call(
+                embed_kernel,
+                [SMEM, SMEM, ANY, ANY],
+                [shape((16, width), bf16)],
+                [
+                    pltpu.VMEM((PAIR, 8, width), bf16),
+                    pltpu.VMEM(time_weight.shape, bf16),
+                    pltpu.SemaphoreType.DMA((PAIR + 1,)),
+                ],
+                PREPARE_LIMIT,
+                some,
+            )(timesteps, labels, table, time_weight)
+            waiting = [embedded]
+            far, embedded = lax.optimization_barrier((far, embedded))
+        elif len(waiting) == 1:
+            operands = (embedded, mod_weight[0], mod_bias, norm_gain)
+            mod_keep, mod_send = call(
+                modulate_kernel,
+                [ANY] * 4,
+                [shape((8, channels), f32)] * 2,
+                [pltpu.VMEM(value.shape, value.dtype) for value in operands] + [pltpu.SemaphoreType.DMA((4,))],
+                PREPARE_LIMIT,
+                some,
+            )(*operands)
+            waiting.append(mod_keep)
+            far, mod_keep, mod_send = lax.optimization_barrier((far, mod_keep, mod_send))
+        far_order = [k ^ bit for k in order]
+        if bit == 1:
+            break
+        near = jnp.concatenate([near, far])
+        order, bit = order + far_order, bit // 2
+    mod_other = lax.ppermute(mod_send, "segment", swap)
+    weights, params = call(
+        layout_kernel,
+        [ANY] * 4,
+        [shape((PAIR, 9 * channels, channels), bf16), shape((8, channels), f32)],
+        [pltpu.VMEM((PAIR, 8, channels), f32), pltpu.SemaphoreType.DMA((2 * PAIR,))],
+        cost=some,
+    )(weight, other_weight, mod_keep, mod_other)
 
     image_shape = shape((sh.pixels, channels), bf16)
     pack_shape = shape((sh.pack, channels), f32)
@@ -452,10 +494,16 @@
         pairs = [(PAIR * source + k, PAIR * target + k) for k in range(PAIR)]
         return lax.ppermute(value, "segment", pairs)
 
-    entering, middles = [image], []
-    for active in range(stages - 1):
+    image, middle, out = call(
+        functools.partial(forward_kernel, sh, 0, (order, far_order)),
+        [VMEM] * 4,
+        [image_shape] * 3,
+        common,
+    )(near, far, params, weights)
+    entering, middles = [image, hop(out, 0, 1)], [middle]
+    for active in range(1, stages - 1):
         middle, out = call(
-            functools.partial(forward_kernel, sh, active),
+            functools.partial(forward_kernel, sh, active, None),
             [VMEM] * 3,
             [image_shape, image_shape],
             common,
@@ -485,6 +533,7 @@
             [VMEM] * 7,
             outs[:2] if last else outs,
             scratch[-1:] + scratch if last else scratch,
+            aliases={5: 0, 6: 1},
         )(entering[active], middles[active], upstream, params, weights, keep, send)
     other = lax.ppermute(send, "segment", swap)
     grads, conv_grad, mod_grad = call(

time: 44.8 us -> 38.8 us (0.87)
  local copies, waits for them, and re-layouts: 7.38 us -> 0.71 us
  Pallas kernels: 8.73 us -> 10.5 us
  starting transfers between devices: 11.2 us -> 10.2 us
  waiting for transfers between devices: 14.8 us -> 15.5 us
  other arithmetic: 1.34 us -> 0.76 us
    all_to_all x1 -> x0, starting transfers between devices: 7.24 us -> none  [shards(): image = lax.all_to_all(copies, 'space', 0, 0).reshape(sh.pixels, channels)]
    unnamed x24 -> x8, local copies, waits for them, and re-layouts: 7.38 us -> 0.71 us
    ppermute x4 -> x5, starting transfers between devices: 1.16 us -> 7.42 us  [the longest x3 6.9 us: shards(): far = lax.ppermute(near, 'space', [(i, i ^ bit) for i in range(spaces)])]
    pallas_call x3 -> x4, Pallas kernels: 5.1 us -> 6.82 us  [the longest x1 2.36 us: shards(): call(embed_kernel, [SMEM, SMEM, ANY, ANY], [shape((16, width), bf16)], [p...]
    ppermute x4 -> x5, waiting for transfers between devices: 0.83 us -> 1.98 us  [the longest x1 1.38 us: shards(): mod_other = lax.ppermute(mod_send, 'segment', swap)]
    select_n x1, other arithmetic: 1.34 us -> 0.74 us  [shards(): ends = jnp.where(stage == 0, x_in, out_cotangent)]
    ppermute x2, waiting for transfers between devices: 12.4 us -> 11.9 us  [hop(): return lax.ppermute(value, 'segment', pairs)]
  transfers between devices with their start and end apart: 8 -> 8, of which waited for: 4 -> 6; matrix products, arithmetic and copies ran while one was open for 3% -> 2% of each run, Pallas kernels for 7% -> 12%
where the time goes in v1:
time: 38.8 us; the launch traced here: 38.4 us
  waiting for transfers between devices  15.5 us (40%)
  Pallas kernels  10.5 us (27%)
  starting transfers between devices  10.2 us (26%)
  other arithmetic  0.76 us (2%)
  between operations  0.73 us (2%)
  local copies, waits for them, and re-layouts  0.71 us (2%)
    ppermute x2, waiting for transfers between devices, hop(): return lax.ppermute(value, 'segment', pairs)  11.9 us
    ppermute x3, starting transfers between devices, shards(): far = lax.ppermute(near, 'space', [(i, i ^ bit) for i in range(spaces)])  6.9 us
    ppermute x2, starting transfers between devices, hop(): return lax.ppermute(value, 'segment', pairs)  2.68 us
    pallas_call x1, Pallas kernels, shards(): call(embed_kernel, [SMEM, SMEM, ANY, ANY], [shape((16, width), bf16)], [p...  2.36 us
    pallas_call x1, Pallas kernels, shards(): call(functools.partial(backward_kernel, sh, active, False), [VMEM] * 7, o...  2.32 us
    pallas_call x1, Pallas kernels, shards(): call(functools.partial(forward_kernel, sh, 0, (order, far_order)), [VMEM]...  2.05 us
    pallas_call x1, Pallas kernels, shards(): call(modulate_kernel, [ANY] * 4, [shape((8, channels), f32)] * 2, [pltpu....  1.88 us
    ppermute x1, waiting for transfers between devices, shards(): other = lax.ppermute(send, 'segment', swap)  1.63 us
  transfers between devices with their start and end apart: 8, of which 6 were waited for; matrix products, arithmetic and copies ran while one was open for 2% of the time, Pallas kernels for 12%

profile of v1, /device:TPU:0, one launch (start us, length us, event | category | flops | bytes accessed | tf_op | source)
XLA Modules:
  0.0 38.4 jit_solution(15886089645735422394)
XLA Ops:
  0.6 0.5 %collective-permute-start.3 = (bf16[2304,256]{1,0:T(8,128)(2,1)}, bf16[2304,256]{1,0:T(8,128)(2,1)S(1)}, u32[]{:S(2)}, u32[]{:S(2)}) collective-permute-start(bf16[2304,256]{1,0:T(8,128)(2,1)} %bitcast.7), channel_id=1, source_target_pairs={{0,8},{8,0},{16,24},{24,16},{1,9},{9,1},{17,25},{25,17},{2,10},{10... | collective-permute-start | bytes 3538952 | tf_op jit(solution)/shard_map/ppermute | solution.py:438
  1.2 0.7 %dynamic-slice_select_fusion = bf16[1,2,16,256]{3,2,1,0:T(8,128)(2,1)S(1)} fusion(bf16[2,2,16,256]{3,2,1,0:T(8,128)(2,1)} %param.11, s32[]{:T(128)S(6)} %select_n.27, bf16[2,2,16,256]{3,2,1,0:T(8,128)(2,1)} %param.10, pred[]{:T(512)S(6)} %eq.5), kind=kLoop, calls=%fused_computation.2 | loop fusion | flops 8192 | bytes 49157 | tf_op jit(solution)/shard_map/jit(_where)/select_n | solution.py:439
  1.9 3.7 %collective-permute-start = (bf16[1,32,256]{2,1,0:T(8,128)(2,1)S(1)}, bf16[1,32,256]{2,1,0:T(8,128)(2,1)S(1)}, u32[]{:S(2)}, u32[]{:S(2)}) collective-permute-start(bf16[1,32,256]{2,1,0:T(8,128)(2,1)S(1)} %bitcast.11), channel_id=1, source_target_pairs={{0,4},{1,5},{2,6},{3,7},{4,0},{5,1},{6,2},{7,3},{8,12},{9,13},{10,... | collective-permute-start | bytes 49160 | tf_op jit(solution)/shard_map/ppermute | solution.py:447
  5.6 2.4 %shard_map.121.embedded_hbm.embedded_ref = bf16[16,512]{1,0:T(8,128)(2,1)} custom-call(s32[2]{0:T(128)} %times_ref.1, s32[2]{0:T(128)} %labels_ref.1, bf16[125,8,512]{2,1,0:T(8,128)(2,1)} %bitcast.9, bf16[128,512]{1,0:T(8,128)(2,1)} %time_weight_hbm.1), custom_call_target="tpu_custom_call" | custom-call | flops 1048576 | bytes 4194304 | tf_op jit(solution)/shard_map/pallas_call | solution.py:449
  8.0 0.0 collective-permute-done
  8.0 1.6 %collective-permute-start.1 = (bf16[2,32,256]{2,1,0:T(8,128)(2,1)S(1)}, bf16[2,32,256]{2,1,0:T(8,128)(2,1)S(1)}, u32[]{:S(2)}, u32[]{:S(2)}) collective-permute-start(bf16[2,32,256]{2,1,0:T(8,128)(2,1)S(1)} %pad_maximum_fusion.1), channel_id=1, source_target_pairs={{0,2},{1,3},{2,0},{3,1},{4,6},{5,7},{6,4},{7,5},{8,10},{9,11},{10,... | collective-permute-start | bytes 98312 | tf_op jit(solution)/shard_map/ppermute | solution.py:447
  9.6 1.9 %shard_map.122 = (f32[8,256]{1,0:T(8,128)}, f32[8,256]{1,0:T(8,128)}) custom-call(bf16[16,512]{1,0:T(8,128)(2,1)} %shard_map.121.embedded_hbm.embedded_ref, bf16[512,512]{1,0:T(8,128)(2,1)} %bitcast.10, f32[1,512]{1,0:T(1,128)} %bias_hbm.1, f32[1,256]{1,0:T(1,128)} %gain_ref.1), custom_call_target="tpu_custom_call" | custom-call | flops 1048576 | bytes 4194304 | tf_op jit(solution)/shard_map/pallas_call | solution.py:465
  11.5 0.4 %collective-permute-done.1 = bf16[2,32,256]{2,1,0:T(8,128)(2,1)S(1)} collective-permute-done((bf16[2,32,256]{2,1,0:T(8,128)(2,1)S(1)}, bf16[2,32,256]{2,1,0:T(8,128)(2,1)S(1)}, u32[]{:S(2)}, u32[]{:S(2)}) %collective-permute-start.1) | collective-permute-done | bytes 32800 | tf_op jit(solution)/shard_map/ppermute | solution.py:447
  12.0 1.6 %collective-permute-start.2 = (bf16[4,32,256]{2,1,0:T(8,128)(2,1)S(1)}, bf16[4,32,256]{2,1,0:T(8,128)(2,1)S(1)}, u32[]{:S(2)}, u32[]{:S(2)}) collective-permute-start(bf16[4,32,256]{2,1,0:T(8,128)(2,1)S(1)} %pad_maximum_fusion.refs_0_), channel_id=1, source_target_pairs={{0,1},{1,0},{2,3},{3,2},{4,5},{5,4},{6,7},{7,6},{8,9},{9,8},{10,11... | collective-permute-start | bytes 196616 | tf_op jit(solution)/shard_map/ppermute | solution.py:447
  13.5 0.0 collective-permute-start.4
  13.5 1.4 %collective-permute-done.4.mod_other_any = f32[8,256]{1,0:T(8,128)S(1)} collective-permute-done((f32[8,256]{1,0:T(8,128)}, f32[8,256]{1,0:T(8,128)S(1)}, u32[]{:S(2)}, u32[]{:S(2)}) %collective-permute-start.4) | collective-permute-done | bytes 8224 | tf_op jit(solution)/shard_map/ppermute | solution.py:480
  14.9 0.0 collective-permute-done.3.other_any
  14.9 0.7 %copy-done.2 = f32[8,256]{1,0:T(8,128)S(1)} copy-done((f32[8,256]{1,0:T(8,128)S(1)}, f32[8,256]{1,0:T(8,128)}, u32[]{:S(2)}) %copy-start.2) | copy-done | bytes 8216
  15.6 0.5 %shard_map.123 = (bf16[2,2304,256]{2,1,0:T(8,128)(2,1)S(1)}, f32[8,256]{1,0:T(8,128)S(1)}) custom-call(bf16[2304,256]{1,0:T(8,128)(2,1)S(1)} %bitcast.8, bf16[2304,256]{1,0:T(8,128)(2,1)S(1)} %collective-permute-done.3.other_any, f32[8,256]{1,0:T(8,128)S(1)} %copy-done.2, f32[8,256]{1,0:T(8,128)S(1)} %collective-permute-done.4.mod_other_any), custom_call_target="tpu_custom_call" | custom-call | flops 1048576 | bytes 4194304 | tf_op jit(solution)/shard_map/pallas_call | solution.py:481
  16.2 0.2 collective-permute-done.2.refs_1_
  16.3 2.1 %shard_map.124 = (bf16[256,256]{1,0:T(8,128)(2,1)S(1)}, bf16[256,256]{1,0:T(8,128)(2,1)S(1)}, bf16[256,256]{1,0:T(8,128)(2,1)S(1)}) custom-call(bf16[4,32,256]{2,1,0:T(8,128)(2,1)S(1)} %pad_maximum_fusion.refs_0_, bf16[4,32,256]{2,1,0:T(8,128)(2,1)S(1)} %collective-permute-done.2.refs_1_, f32[8,256]{1,0:T(8,128)S(1)} %get-tuple-element.30.refs_2_.refs_3_, ...), custom_call_target="tpu_custom_call" | custom-call | tf_op jit(solution)/shard_map/pallas_call | solution.py:497
  18.4 1.4 %collective-permute-start.5 = (bf16[256,256]{1,0:T(8,128)(2,1)S(1)}, bf16[256,256]{1,0:T(8,128)(2,1)S(1)}, u32[]{:S(2)}, u32[]{:S(2)}) collective-permute-start(bf16[256,256]{1,0:T(8,128)(2,1)S(1)} %get-tuple-element.34), channel_id=1, source_target_pairs={{0,16},{8,24},{1,17},{9,25},{2,18},{10,26},{3,19},{11,27},{4,20},{... | collective-permute-start | bytes 393224 | tf_op jit(solution)/shard_map/ppermute | solution.py:495
  19.8 3.1 %collective-permute-done.5.refs_0_ = bf16[256,256]{1,0:T(8,128)(2,1)S(1)} collective-permute-done((bf16[256,256]{1,0:T(8,128)(2,1)S(1)}, bf16[256,256]{1,0:T(8,128)(2,1)S(1)}, u32[]{:S(2)}, u32[]{:S(2)}) %collective-permute-start.5) | collective-permute-done | bytes 131104 | tf_op jit(solution)/shard_map/ppermute | solution.py:495
  22.9 1.3 %collective-permute-start.6 = (bf16[256,256]{1,0:T(8,128)(2,1)S(1)}, bf16[256,256]{1,0:T(8,128)(2,1)S(1)}, u32[]{:S(2)}, u32[]{:S(2)}) collective-permute-start(bf16[256,256]{1,0:T(8,128)(2,1)S(1)} %get-tuple-element.35), channel_id=1, source_target_pairs={{16,0},{24,8},{17,1},{25,9},{18,2},{26,10},{19,3},{27,11},{20,4},{... | collective-permute-start | bytes 393224 | tf_op jit(solution)/shard_map/ppermute | solution.py:495
  24.2 8.8 %collective-permute-done.6.refs_2_ = bf16[256,256]{1,0:T(8,128)(2,1)S(1)} collective-permute-done((bf16[256,256]{1,0:T(8,128)(2,1)S(1)}, bf16[256,256]{1,0:T(8,128)(2,1)S(1)}, u32[]{:S(2)}, u32[]{:S(2)}) %collective-permute-start.6) | collective-permute-done | bytes 131104 | tf_op jit(solution)/shard_map/ppermute | solution.py:495
  33.0 2.3 %shard_map.126 = (f32[328,256]{1,0:T(8,128)S(1)}, f32[328,256]{1,0:T(8,128)S(1)}) custom-call(bf16[256,256]{1,0:T(8,128)(2,1)S(1)} %get-tuple-element.32.refs_1_.refs_0_, bf16[256,256]{1,0:T(8,128)(2,1)S(1)} %get-tuple-element.33.refs_1_, bf16[256,256]{1,0:T(8,128)(2,1)S(1)} %collective-permute-done.6.refs_2_, ...), custom_call_target="tpu_custom_call", output_to_operand_aliasing={{0}: (5, {}), {1}: (6, {})} | custom-call | tf_op jit(solution)/shard_map/pallas_call | solution.py:531
  35.3 0.1 collective-permute-start.7
  35.4 1.6 %collective-permute-done.7.other_ref = f32[328,256]{1,0:T(8,128)S(1)} collective-permute-done((f32[328,256]{1,0:T(8,128)S(1)}, f32[328,256]{1,0:T(8,128)S(1)}, u32[]{:S(2)}, u32[]{:S(2)}) %collective-permute-start.7) | collective-permute-done | bytes 335904 | tf_op jit(solution)/shard_map/ppermute | solution.py:538
  37.0 1.4 %shard_map.127 = (bf16[2,32,256]{2,1,0:T(8,128)(2,1)}, f32[288,256]{1,0:T(8,128)}, f32[512,512]{1,0:T(8,128)}) custom-call(f32[328,256]{1,0:T(8,128)S(1)} %get-tuple-element.38.keep_ref, f32[328,256]{1,0:T(8,128)S(1)} %collective-permute-done.7.other_ref, bf16[16,512]{1,0:T(8,128)(2,1)S(1)} %copy-done.1, f32[1,256]{1,0:T(1,128)S(1)} %copy-done.3), custom_call_target="tpu_custom_call" | custom-call | tf_op jit(solution)/shard_map/pallas_call | solution.py:539
  (10 shorter events, 0.0 us)
Async XLA Ops:
  0.6 14.3 %copy-start = (bf16[1,3,3,256,256]{4,3,2,1,0:T(8,128)(2,1)S(1)}, bf16[1,3,3,256,256]{4,3,2,1,0:T(8,128)(2,1)}, u32[]{:S(2)}) copy-start(bf16[1,3,3,256,256]{4,3,2,1,0:T(8,128)(2,1)} %param.16) | copy-start | bytes 3538948
  0.6 14.3 %collective-permute-start.3 = (bf16[2304,256]{1,0:T(8,128)(2,1)}, bf16[2304,256]{1,0:T(8,128)(2,1)S(1)}, u32[]{:S(2)}, u32[]{:S(2)}) collective-permute-start(bf16[2304,256]{1,0:T(8,128)(2,1)} %bitcast.7), channel_id=1, source_target_pairs={{0,8},{8,0},{16,24},{24,16},{1,9},{9,1},{17,25},{25,17},{2,10},{10... | collective-permute-start | bytes 3538952 | tf_op jit(solution)/shard_map/ppermute | solution.py:438
  1.9 6.1 %collective-permute-start = (bf16[1,32,256]{2,1,0:T(8,128)(2,1)S(1)}, bf16[1,32,256]{2,1,0:T(8,128)(2,1)S(1)}, u32[]{:S(2)}, u32[]{:S(2)}) collective-permute-start(bf16[1,32,256]{2,1,0:T(8,128)(2,1)S(1)} %bitcast.11), channel_id=1, source_target_pairs={{0,4},{1,5},{2,6},{3,7},{4,0},{5,1},{6,2},{7,3},{8,12},{9,13},{10,... | collective-permute-start | bytes 49160 | tf_op jit(solution)/shard_map/ppermute | solution.py:447
  8.0 4.0 %collective-permute-start.1 = (bf16[2,32,256]{2,1,0:T(8,128)(2,1)S(1)}, bf16[2,32,256]{2,1,0:T(8,128)(2,1)S(1)}, u32[]{:S(2)}, u32[]{:S(2)}) collective-permute-start(bf16[2,32,256]{2,1,0:T(8,128)(2,1)S(1)} %pad_maximum_fusion.1), channel_id=1, source_target_pairs={{0,2},{1,3},{2,0},{3,1},{4,6},{5,7},{6,4},{7,5},{8,10},{9,11},{10,... | collective-permute-start | bytes 98312 | tf_op jit(solution)/shard_map/ppermute | solution.py:447
  12.0 4.3 %collective-permute-start.2 = (bf16[4,32,256]{2,1,0:T(8,128)(2,1)S(1)}, bf16[4,32,256]{2,1,0:T(8,128)(2,1)S(1)}, u32[]{:S(2)}, u32[]{:S(2)}) collective-permute-start(bf16[4,32,256]{2,1,0:T(8,128)(2,1)S(1)} %pad_maximum_fusion.refs_0_), channel_id=1, source_target_pairs={{0,1},{1,0},{2,3},{3,2},{4,5},{5,4},{6,7},{7,6},{8,9},{9,8},{10,11... | collective-permute-start | bytes 196616 | tf_op jit(solution)/shard_map/ppermute | solution.py:447
  13.5 1.4 %collective-permute-start.4 = (f32[8,256]{1,0:T(8,128)}, f32[8,256]{1,0:T(8,128)S(1)}, u32[]{:S(2)}, u32[]{:S(2)}) collective-permute-start(f32[8,256]{1,0:T(8,128)} %get-tuple-element.29), channel_id=1, source_target_pairs={{0,8},{8,0},{16,24},{24,16},{1,9},{9,1},{17,25},{25,17},{2,10},{10... | collective-permute-start | bytes 24584 | tf_op jit(solution)/shard_map/ppermute | solution.py:480
  14.9 0.7 %copy-start.2 = (f32[8,256]{1,0:T(8,128)S(1)}, f32[8,256]{1,0:T(8,128)}, u32[]{:S(2)}) copy-start(f32[8,256]{1,0:T(8,128)} %get-tuple-element.28.mod_keep_any) | copy-start | bytes 24580
  18.4 4.5 %collective-permute-start.5 = (bf16[256,256]{1,0:T(8,128)(2,1)S(1)}, bf16[256,256]{1,0:T(8,128)(2,1)S(1)}, u32[]{:S(2)}, u32[]{:S(2)}) collective-permute-start(bf16[256,256]{1,0:T(8,128)(2,1)S(1)} %get-tuple-element.34), channel_id=1, source_target_pairs={{0,16},{8,24},{1,17},{9,25},{2,18},{10,26},{3,19},{11,27},{4,20},{... | collective-permute-start | bytes 393224 | tf_op jit(solution)/shard_map/ppermute | solution.py:495
  22.9 10.1 %collective-permute-start.6 = (bf16[256,256]{1,0:T(8,128)(2,1)S(1)}, bf16[256,256]{1,0:T(8,128)(2,1)S(1)}, u32[]{:S(2)}, u32[]{:S(2)}) collective-permute-start(bf16[256,256]{1,0:T(8,128)(2,1)S(1)} %get-tuple-element.35), channel_id=1, source_target_pairs={{16,0},{24,8},{17,1},{25,9},{18,2},{26,10},{19,3},{27,11},{20,4},{... | collective-permute-start | bytes 393224 | tf_op jit(solution)/shard_map/ppermute | solution.py:495
  32.9 4.0 %copy-start.1 = (bf16[16,512]{1,0:T(8,128)(2,1)S(1)}, bf16[16,512]{1,0:T(8,128)(2,1)}, u32[]{:S(2)}) copy-start(bf16[16,512]{1,0:T(8,128)(2,1)} %shard_map.121.embedded_hbm.embedded_ref) | copy-start | bytes 49156
  33.0 4.0 %copy-start.3 = (f32[1,256]{1,0:T(1,128)S(1)}, f32[1,256]{1,0:T(1,128)}, u32[]{:S(2)}) copy-start(f32[1,256]{1,0:T(1,128)} %gain_ref.1) | copy-start | bytes 3076
  35.3 1.7 %collective-permute-start.7 = (f32[328,256]{1,0:T(8,128)S(1)}, f32[328,256]{1,0:T(8,128)S(1)}, u32[]{:S(2)}, u32[]{:S(2)}) collective-permute-start(f32[328,256]{1,0:T(8,128)S(1)} %get-tuple-element.39), channel_id=1, source_target_pairs={{0,8},{8,0},{16,24},{24,16},{1,9},{9,1},{17,25},{25,17},{2,10},{10... | collective-permute-start | bytes 1007624 | tf_op jit(solution)/shard_map/ppermute | solution.py:538

commit v2 on v1

--- a/solution.py
+++ b/solution.py
@@ -492,7 +492,7 @@
 
     def hop(value, source, target):
         pairs = [(PAIR * source + k, PAIR * target + k) for k in range(PAIR)]
-        return lax.ppermute(value, "segment", pairs)
+        return lax.ppermute(value, "segment", pairs + [(b, a) for a, b in pairs])
 
     image, middle, out = call(
         functools.partial(forward_kernel, sh, 0, (order, far_order)),

time: 38.8 us -> 36.4 us (0.938)
  waiting for transfers between devices: 15.5 us -> 12.2 us
  starting transfers between devices: 10.2 us -> 11.2 us
    ppermute x2, waiting for transfers between devices: 11.9 us -> 8.59 us  [hop(): return lax.ppermute(value, 'segment', pairs + [(b, a) for a, b in pairs])]
    ppermute x2, starting transfers between devices: 2.68 us -> 3.66 us  [hop(): return lax.ppermute(value, 'segment', pairs + [(b, a) for a, b in pairs])]
  transfers between devices with their start and end apart: 8 -> 8, of which waited for: 6 -> 6; matrix products, arithmetic and copies ran while one was open for 2% -> 2% of each run, Pallas kernels for 12% -> 13%
where the time goes in v2:
time: 36.4 us; the launch traced here: 36 us
  waiting for transfers between devices  12.2 us (34%)
  starting transfers between devices  11.2 us (31%)
  Pallas kernels  10.5 us (29%)
  other arithmetic  0.76 us (2%)
  between operations  0.73 us (2%)
  local copies, waits for them, and re-layouts  0.71 us (2%)
    ppermute x2, waiting for transfers between devices, hop(): return lax.ppermute(value, 'segment', pairs + [(b, a) for a, b in pairs])  8.59 us
    ppermute x3, starting transfers between devices, shards(): far = lax.ppermute(near, 'space', [(i, i ^ bit) for i in range(spaces)])  6.9 us
    ppermute x2, starting transfers between devices, hop(): return lax.ppermute(value, 'segment', pairs + [(b, a) for a, b in pairs])  3.66 us
    pallas_call x1, Pallas kernels, shards(): call(embed_kernel, [SMEM, SMEM, ANY, ANY], [shape((16, width), bf16)], [p...  2.36 us
    pallas_call x1, Pallas kernels, shards(): call(functools.partial(backward_kernel, sh, active, False), [VMEM] * 7, o...  2.32 us
    pallas_call x1, Pallas kernels, shards(): call(functools.partial(forward_kernel, sh, 0, (order, far_order)), [VMEM]...  2.05 us
    pallas_call x1, Pallas kernels, shards(): call(modulate_kernel, [ANY] * 4, [shape((8, channels), f32)] * 2, [pltpu....  1.88 us
    ppermute x1, waiting for transfers between devices, shards(): other = lax.ppermute(send, 'segment', swap)  1.63 us
  transfers between devices with their start and end apart: 8, of which 6 were waited for; matrix products, arithmetic and copies ran while one was open for 2% of the time, Pallas kernels for 13%

profile of v2, /device:TPU:0, one launch (start us, length us, event | category | flops | bytes accessed | tf_op | source)
XLA Modules:
  0.0 36.0 jit_solution(3076133558762030705)
XLA Ops:
  0.6 0.5 %collective-permute-start.3 = (bf16[2304,256]{1,0:T(8,128)(2,1)}, bf16[2304,256]{1,0:T(8,128)(2,1)S(1)}, u32[]{:S(2)}, u32[]{:S(2)}) collective-permute-start(bf16[2304,256]{1,0:T(8,128)(2,1)} %bitcast.7), channel_id=1, source_target_pairs={{0,8},{8,0},{16,24},{24,16},{1,9},{9,1},{17,25},{25,17},{2,10},{10... | collective-permute-start | bytes 3538952 | tf_op jit(solution)/shard_map/ppermute | solution.py:438
  1.2 0.7 %dynamic-slice_select_fusion = bf16[1,2,16,256]{3,2,1,0:T(8,128)(2,1)S(1)} fusion(bf16[2,2,16,256]{3,2,1,0:T(8,128)(2,1)} %param.11, s32[]{:T(128)S(6)} %select_n.27, bf16[2,2,16,256]{3,2,1,0:T(8,128)(2,1)} %param.10, pred[]{:T(512)S(6)} %eq.5), kind=kLoop, calls=%fused_computation.2 | loop fusion | flops 8192 | bytes 49157 | tf_op jit(solution)/shard_map/jit(_where)/select_n | solution.py:439
  1.9 3.7 %collective-permute-start = (bf16[1,32,256]{2,1,0:T(8,128)(2,1)S(1)}, bf16[1,32,256]{2,1,0:T(8,128)(2,1)S(1)}, u32[]{:S(2)}, u32[]{:S(2)}) collective-permute-start(bf16[1,32,256]{2,1,0:T(8,128)(2,1)S(1)} %bitcast.11), channel_id=1, source_target_pairs={{0,4},{1,5},{2,6},{3,7},{4,0},{5,1},{6,2},{7,3},{8,12},{9,13},{10,... | collective-permute-start | bytes 49160 | tf_op jit(solution)/shard_map/ppermute | solution.py:447
  5.6 2.4 %shard_map.121.embedded_hbm.embedded_ref = bf16[16,512]{1,0:T(8,128)(2,1)} custom-call(s32[2]{0:T(128)} %times_ref.1, s32[2]{0:T(128)} %labels_ref.1, bf16[125,8,512]{2,1,0:T(8,128)(2,1)} %bitcast.9, bf16[128,512]{1,0:T(8,128)(2,1)} %time_weight_hbm.1), custom_call_target="tpu_custom_call" | custom-call | flops 1048576 | bytes 4194304 | tf_op jit(solution)/shard_map/pallas_call | solution.py:449
  8.0 0.0 collective-permute-done
  8.0 1.6 %collective-permute-start.1 = (bf16[2,32,256]{2,1,0:T(8,128)(2,1)S(1)}, bf16[2,32,256]{2,1,0:T(8,128)(2,1)S(1)}, u32[]{:S(2)}, u32[]{:S(2)}) collective-permute-start(bf16[2,32,256]{2,1,0:T(8,128)(2,1)S(1)} %pad_maximum_fusion.1), channel_id=1, source_target_pairs={{0,2},{1,3},{2,0},{3,1},{4,6},{5,7},{6,4},{7,5},{8,10},{9,11},{10,... | collective-permute-start | bytes 98312 | tf_op jit(solution)/shard_map/ppermute | solution.py:447
  9.6 1.9 %shard_map.122 = (f32[8,256]{1,0:T(8,128)}, f32[8,256]{1,0:T(8,128)}) custom-call(bf16[16,512]{1,0:T(8,128)(2,1)} %shard_map.121.embedded_hbm.embedded_ref, bf16[512,512]{1,0:T(8,128)(2,1)} %bitcast.10, f32[1,512]{1,0:T(1,128)} %bias_hbm.1, f32[1,256]{1,0:T(1,128)} %gain_ref.1), custom_call_target="tpu_custom_call" | custom-call | flops 1048576 | bytes 4194304 | tf_op jit(solution)/shard_map/pallas_call | solution.py:465
  11.5 0.4 %collective-permute-done.1 = bf16[2,32,256]{2,1,0:T(8,128)(2,1)S(1)} collective-permute-done((bf16[2,32,256]{2,1,0:T(8,128)(2,1)S(1)}, bf16[2,32,256]{2,1,0:T(8,128)(2,1)S(1)}, u32[]{:S(2)}, u32[]{:S(2)}) %collective-permute-start.1) | collective-permute-done | bytes 32800 | tf_op jit(solution)/shard_map/ppermute | solution.py:447
  12.0 1.6 %collective-permute-start.2 = (bf16[4,32,256]{2,1,0:T(8,128)(2,1)S(1)}, bf16[4,32,256]{2,1,0:T(8,128)(2,1)S(1)}, u32[]{:S(2)}, u32[]{:S(2)}) collective-permute-start(bf16[4,32,256]{2,1,0:T(8,128)(2,1)S(1)} %pad_maximum_fusion.refs_0_), channel_id=1, source_target_pairs={{0,1},{1,0},{2,3},{3,2},{4,5},{5,4},{6,7},{7,6},{8,9},{9,8},{10,11... | collective-permute-start | bytes 196616 | tf_op jit(solution)/shard_map/ppermute | solution.py:447
  13.5 0.0 collective-permute-start.4
  13.5 1.4 %collective-permute-done.4.mod_other_any = f32[8,256]{1,0:T(8,128)S(1)} collective-permute-done((f32[8,256]{1,0:T(8,128)}, f32[8,256]{1,0:T(8,128)S(1)}, u32[]{:S(2)}, u32[]{:S(2)}) %collective-permute-start.4) | collective-permute-done | bytes 8224 | tf_op jit(solution)/shard_map/ppermute | solution.py:480
  14.9 0.0 collective-permute-done.3.other_any
  14.9 0.7 %copy-done.2 = f32[8,256]{1,0:T(8,128)S(1)} copy-done((f32[8,256]{1,0:T(8,128)S(1)}, f32[8,256]{1,0:T(8,128)}, u32[]{:S(2)}) %copy-start.2) | copy-done | bytes 8216
  15.6 0.5 %shard_map.123 = (bf16[2,2304,256]{2,1,0:T(8,128)(2,1)S(1)}, f32[8,256]{1,0:T(8,128)S(1)}) custom-call(bf16[2304,256]{1,0:T(8,128)(2,1)S(1)} %bitcast.8, bf16[2304,256]{1,0:T(8,128)(2,1)S(1)} %collective-permute-done.3.other_any, f32[8,256]{1,0:T(8,128)S(1)} %copy-done.2, f32[8,256]{1,0:T(8,128)S(1)} %collective-permute-done.4.mod_other_any), custom_call_target="tpu_custom_call" | custom-call | flops 1048576 | bytes 4194304 | tf_op jit(solution)/shard_map/pallas_call | solution.py:481
  16.2 0.2 collective-permute-done.2.refs_1_
  16.3 2.1 %shard_map.124 = (bf16[256,256]{1,0:T(8,128)(2,1)S(1)}, bf16[256,256]{1,0:T(8,128)(2,1)S(1)}, bf16[256,256]{1,0:T(8,128)(2,1)S(1)}) custom-call(bf16[4,32,256]{2,1,0:T(8,128)(2,1)S(1)} %pad_maximum_fusion.refs_0_, bf16[4,32,256]{2,1,0:T(8,128)(2,1)S(1)} %collective-permute-done.2.refs_1_, f32[8,256]{1,0:T(8,128)S(1)} %get-tuple-element.30.refs_2_.refs_3_, ...), custom_call_target="tpu_custom_call" | custom-call | tf_op jit(solution)/shard_map/pallas_call | solution.py:497
  18.4 0.1 collective-permute-start.5
  18.5 5.4 %collective-permute-done.5.refs_0_ = bf16[256,256]{1,0:T(8,128)(2,1)S(1)} collective-permute-done((bf16[256,256]{1,0:T(8,128)(2,1)S(1)}, bf16[256,256]{1,0:T(8,128)(2,1)S(1)}, u32[]{:S(2)}, u32[]{:S(2)}) %collective-permute-start.5) | collective-permute-done | bytes 131104 | tf_op jit(solution)/shard_map/ppermute | solution.py:495
  23.9 3.6 %collective-permute-start.6 = (bf16[256,256]{1,0:T(8,128)(2,1)S(1)}, bf16[256,256]{1,0:T(8,128)(2,1)S(1)}, u32[]{:S(2)}, u32[]{:S(2)}) collective-permute-start(bf16[256,256]{1,0:T(8,128)(2,1)S(1)} %get-tuple-element.35), channel_id=1, source_target_pairs={{16,0},{24,8},{0,16},{8,24},{17,1},{25,9},{1,17},{9,25},{18,2},{26... | collective-permute-start | bytes 393224 | tf_op jit(solution)/shard_map/ppermute | solution.py:495
  27.5 3.2 %collective-permute-done.6.refs_2_ = bf16[256,256]{1,0:T(8,128)(2,1)S(1)} collective-permute-done((bf16[256,256]{1,0:T(8,128)(2,1)S(1)}, bf16[256,256]{1,0:T(8,128)(2,1)S(1)}, u32[]{:S(2)}, u32[]{:S(2)}) %collective-permute-start.6) | collective-permute-done | bytes 131104 | tf_op jit(solution)/shard_map/ppermute | solution.py:495
  30.6 2.3 %shard_map.126 = (f32[328,256]{1,0:T(8,128)S(1)}, f32[328,256]{1,0:T(8,128)S(1)}) custom-call(bf16[256,256]{1,0:T(8,128)(2,1)S(1)} %get-tuple-element.32.refs_1_.refs_0_, bf16[256,256]{1,0:T(8,128)(2,1)S(1)} %get-tuple-element.33.refs_1_, bf16[256,256]{1,0:T(8,128)(2,1)S(1)} %collective-permute-done.6.refs_2_, ...), custom_call_target="tpu_custom_call", output_to_operand_aliasing={{0}: (5, {}), {1}: (6, {})} | custom-call | tf_op jit(solution)/shard_map/pallas_call | solution.py:531
  33.0 0.1 collective-permute-start.7
  33.1 1.6 %collective-permute-done.7.other_ref = f32[328,256]{1,0:T(8,128)S(1)} collective-permute-done((f32[328,256]{1,0:T(8,128)S(1)}, f32[328,256]{1,0:T(8,128)S(1)}, u32[]{:S(2)}, u32[]{:S(2)}) %collective-permute-start.7) | collective-permute-done | bytes 335904 | tf_op jit(solution)/shard_map/ppermute | solution.py:538
  34.7 1.4 %shard_map.127 = (bf16[2,32,256]{2,1,0:T(8,128)(2,1)}, f32[288,256]{1,0:T(8,128)}, f32[512,512]{1,0:T(8,128)}) custom-call(f32[328,256]{1,0:T(8,128)S(1)} %get-tuple-element.38.keep_ref, f32[328,256]{1,0:T(8,128)S(1)} %collective-permute-done.7.other_ref, bf16[16,512]{1,0:T(8,128)(2,1)S(1)} %copy-done.1, f32[1,256]{1,0:T(1,128)S(1)} %copy-done.3), custom_call_target="tpu_custom_call" | custom-call | tf_op jit(solution)/shard_map/pallas_call | solution.py:539
  (10 shorter events, 0.0 us)
Async XLA Ops:
  0.6 14.3 %copy-start = (bf16[1,3,3,256,256]{4,3,2,1,0:T(8,128)(2,1)S(1)}, bf16[1,3,3,256,256]{4,3,2,1,0:T(8,128)(2,1)}, u32[]{:S(2)}) copy-start(bf16[1,3,3,256,256]{4,3,2,1,0:T(8,128)(2,1)} %param.16) | copy-start | bytes 3538948
  0.6 14.3 %collective-permute-start.3 = (bf16[2304,256]{1,0:T(8,128)(2,1)}, bf16[2304,256]{1,0:T(8,128)(2,1)S(1)}, u32[]{:S(2)}, u32[]{:S(2)}) collective-permute-start(bf16[2304,256]{1,0:T(8,128)(2,1)} %bitcast.7), channel_id=1, source_target_pairs={{0,8},{8,0},{16,24},{24,16},{1,9},{9,1},{17,25},{25,17},{2,10},{10... | collective-permute-start | bytes 3538952 | tf_op jit(solution)/shard_map/ppermute | solution.py:438
  1.9 6.1 %collective-permute-start = (bf16[1,32,256]{2,1,0:T(8,128)(2,1)S(1)}, bf16[1,32,256]{2,1,0:T(8,128)(2,1)S(1)}, u32[]{:S(2)}, u32[]{:S(2)}) collective-permute-start(bf16[1,32,256]{2,1,0:T(8,128)(2,1)S(1)} %bitcast.11), channel_id=1, source_target_pairs={{0,4},{1,5},{2,6},{3,7},{4,0},{5,1},{6,2},{7,3},{8,12},{9,13},{10,... | collective-permute-start | bytes 49160 | tf_op jit(solution)/shard_map/ppermute | solution.py:447
  8.0 4.0 %collective-permute-start.1 = (bf16[2,32,256]{2,1,0:T(8,128)(2,1)S(1)}, bf16[2,32,256]{2,1,0:T(8,128)(2,1)S(1)}, u32[]{:S(2)}, u32[]{:S(2)}) collective-permute-start(bf16[2,32,256]{2,1,0:T(8,128)(2,1)S(1)} %pad_maximum_fusion.1), channel_id=1, source_target_pairs={{0,2},{1,3},{2,0},{3,1},{4,6},{5,7},{6,4},{7,5},{8,10},{9,11},{10,... | collective-permute-start | bytes 98312 | tf_op jit(solution)/shard_map/ppermute | solution.py:447
  12.0 4.3 %collective-permute-start.2 = (bf16[4,32,256]{2,1,0:T(8,128)(2,1)S(1)}, bf16[4,32,256]{2,1,0:T(8,128)(2,1)S(1)}, u32[]{:S(2)}, u32[]{:S(2)}) collective-permute-start(bf16[4,32,256]{2,1,0:T(8,128)(2,1)S(1)} %pad_maximum_fusion.refs_0_), channel_id=1, source_target_pairs={{0,1},{1,0},{2,3},{3,2},{4,5},{5,4},{6,7},{7,6},{8,9},{9,8},{10,11... | collective-permute-start | bytes 196616 | tf_op jit(solution)/shard_map/ppermute | solution.py:447
  13.5 1.4 %collective-permute-start.4 = (f32[8,256]{1,0:T(8,128)}, f32[8,256]{1,0:T(8,128)S(1)}, u32[]{:S(2)}, u32[]{:S(2)}) collective-permute-start(f32[8,256]{1,0:T(8,128)} %get-tuple-element.29), channel_id=1, source_target_pairs={{0,8},{8,0},{16,24},{24,16},{1,9},{9,1},{17,25},{25,17},{2,10},{10... | collective-permute-start | bytes 24584 | tf_op jit(solution)/shard_map/ppermute | solution.py:480
  14.9 0.7 %copy-start.2 = (f32[8,256]{1,0:T(8,128)S(1)}, f32[8,256]{1,0:T(8,128)}, u32[]{:S(2)}) copy-start(f32[8,256]{1,0:T(8,128)} %get-tuple-element.28.mod_keep_any) | copy-start | bytes 24580
  18.4 5.5 %collective-permute-start.5 = (bf16[256,256]{1,0:T(8,128)(2,1)S(1)}, bf16[256,256]{1,0:T(8,128)(2,1)S(1)}, u32[]{:S(2)}, u32[]{:S(2)}) collective-permute-start(bf16[256,256]{1,0:T(8,128)(2,1)S(1)} %get-tuple-element.34), channel_id=1, source_target_pairs={{0,16},{8,24},{16,0},{24,8},{1,17},{9,25},{17,1},{25,9},{2,18},{10... | collective-permute-start | bytes 393224 | tf_op jit(solution)/shard_map/ppermute | solution.py:495
  23.9 6.8 %collective-permute-start.6 = (bf16[256,256]{1,0:T(8,128)(2,1)S(1)}, bf16[256,256]{1,0:T(8,128)(2,1)S(1)}, u32[]{:S(2)}, u32[]{:S(2)}) collective-permute-start(bf16[256,256]{1,0:T(8,128)(2,1)S(1)} %get-tuple-element.35), channel_id=1, source_target_pairs={{16,0},{24,8},{0,16},{8,24},{17,1},{25,9},{1,17},{9,25},{18,2},{26... | collective-permute-start | bytes 393224 | tf_op jit(solution)/shard_map/ppermute | solution.py:495
  30.6 4.0 %copy-start.1 = (bf16[16,512]{1,0:T(8,128)(2,1)S(1)}, bf16[16,512]{1,0:T(8,128)(2,1)}, u32[]{:S(2)}) copy-start(bf16[16,512]{1,0:T(8,128)(2,1)} %shard_map.121.embedded_hbm.embedded_ref) | copy-start | bytes 49156
  30.6 4.0 %copy-start.3 = (f32[1,256]{1,0:T(1,128)S(1)}, f32[1,256]{1,0:T(1,128)}, u32[]{:S(2)}) copy-start(f32[1,256]{1,0:T(1,128)} %gain_ref.1) | copy-start | bytes 3076
  33.0 1.7 %collective-permute-start.7 = (f32[328,256]{1,0:T(8,128)S(1)}, f32[328,256]{1,0:T(8,128)S(1)}, u32[]{:S(2)}, u32[]{:S(2)}) collective-permute-start(f32[328,256]{1,0:T(8,128)S(1)} %get-tuple-element.39), channel_id=1, source_target_pairs={{0,8},{8,0},{16,24},{24,16},{1,9},{9,1},{17,25},{25,17},{2,10},{10... | collective-permute-start | bytes 1007624 | tf_op jit(solution)/shard_map/ppermute | solution.py:538

commit v3 on v2

--- a/solution.py
+++ b/solution.py
@@ -269,10 +269,12 @@
     return copies
 
 
-def embed_kernel(times_ref, labels_ref, table_hbm, time_weight_hbm, embedded_ref, table_ref, time_weight_ref, sems):
-    pairs = [(time_weight_hbm, time_weight_ref)]
-    pairs += [(table_hbm.at[pl.ds(labels_ref[i] // 8, 1)], table_ref.at[pl.ds(i, 1)]) for i in range(PAIR)]
-    copies = start_all(pairs, sems)
+def prepare_kernel(times_ref, labels_ref, table_hbm, *refs):
+    sources, (embedded_ref, keep_ref, send_ref), scratch = refs[:4], refs[4:7], refs[7:]
+    time_weight_ref, mod_weight_ref, bias_ref, gain_ref, table_ref, sems = scratch
+    core = lax.axis_index("segment") % PAIR
+    pairs = [(table_hbm.at[pl.ds(labels_ref[i] // 8, 1)], table_ref.at[pl.ds(i, 1)]) for i in range(PAIR)]
+    copies = start_all(pairs + list(zip(sources, scratch[:4])), sems)
     spot = lax.broadcasted_iota(jnp.int32, (16, 1), 0)
     time = jnp.where(spot % 2 == 0, times_ref[0], times_ref[1]).astype(jnp.float32)
     sinusoid = sinusoid_of(time, time_weight_ref.shape[0])
@@ -282,20 +284,15 @@
         row = lax.broadcasted_iota(jnp.int32, block.shape, 0)
         return column(jnp.where(row == labels_ref[image] % 8, block, 0.0))
 
-    for copy in copies:
+    for copy in copies[: PAIR + 1]:
         copy.wait()
     timed = jnp.dot(sinusoid, time_weight_ref[...], preferred_element_type=jnp.float32)
     timed = timed + jnp.where(spot % 2 == 0, label_row(0), label_row(1))
-    embedded_ref[...] = (timed * sigmoid(timed)).astype(jnp.bfloat16)
-
-
-def modulate_kernel(embedded_hbm, mod_weight_hbm, bias_hbm, gain_hbm, keep_ref, send_ref, *scratch):
-    embedded_ref, mod_weight_ref, bias_ref, gain_ref, sems = scratch
-    core = lax.axis_index("segment") % PAIR
-    copies = start_all(zip((embedded_hbm, mod_weight_hbm, bias_hbm, gain_hbm), scratch[:4]), sems)
-    for copy in copies:
+    embedded = (timed * sigmoid(timed)).astype(jnp.bfloat16)
+    embedded_ref[...] = embedded
+    for copy in copies[PAIR + 1 :]:
         copy.wait()
-    modulation = jnp.dot(embedded_ref[...], mod_weight_ref[...], preferred_element_type=jnp.float32) + bias_ref[...]
+    modulation = jnp.dot(embedded, mod_weight_ref[...], preferred_element_type=jnp.float32) + bias_ref[...]
     channels = gain_ref.shape[1]
     factor = gain_ref[...] * (1.0 + modulation[:, :channels])
     shift = modulation[:, channels:]
@@ -441,42 +438,32 @@
     table = label_table.reshape(-1, 8, label_table.shape[1])
     width = time_weight.shape[1]
     some = pl.CostEstimate(flops=1 << 20, bytes_accessed=4 << 20, transcendentals=0)
-    order, bit = [0], spaces // 2
-    waiting = []
+    operands = (time_weight, mod_weight[0], mod_bias, norm_gain)
+    embedded, mod_keep, mod_send = call(
+        prepare_kernel,
+        [SMEM, SMEM] + [ANY] * 5,
+        [shape((16, width), bf16)] + [shape((8, channels), f32)] * 2,
+        [pltpu.VMEM(value.shape, value.dtype) for value in operands]
+        + [pltpu.VMEM((PAIR, 8, width), bf16), pltpu.SemaphoreType.DMA((PAIR + 4,))],
+        PREPARE_LIMIT,
+        some,
+    )(timesteps, labels, table, *operands)
+
+    def exchange(bits):
+        return lax.ppermute(near, "space", [(i, i ^ bits) for i in range(spaces)])
+
+    quarter = spaces // 4
+    order = [k * quarter for k in (0, 3, 2, 1)]
+    fars = [exchange(bits) for bits in order[1:]]
+    *fars, mod_keep, mod_send = lax.optimization_barrier((*fars, mod_keep, mod_send))
+    bit = quarter // 2
+    near = jnp.concatenate([near, *fars])
     while True:
-        far = lax.ppermute(near, "space", [(i, i ^ bit) for i in range(spaces)])
-        if not waiting:
-            (embedded,) = call(
-                embed_kernel,
-                [SMEM, SMEM, ANY, ANY],
-                [shape((16, width), bf16)],
-                [
-                    pltpu.VMEM((PAIR, 8, width), bf16),
-                    pltpu.VMEM(time_weight.shape, bf16),
-                    pltpu.SemaphoreType.DMA((PAIR + 1,)),
-                ],
-                PREPARE_LIMIT,
-                some,
-            )(timesteps, labels, table, time_weight)
-            waiting = [embedded]
-            far, embedded = lax.optimization_barrier((far, embedded))
-        elif len(waiting) == 1:
-            operands = (embedded, mod_weight[0], mod_bias, norm_gain)
-            mod_keep, mod_send = call(
-                modulate_kernel,
-                [ANY] * 4,
-                [shape((8, channels), f32)] * 2,
-                [pltpu.VMEM(value.shape, value.dtype) for value in operands] + [pltpu.SemaphoreType.DMA((4,))],
-                PREPARE_LIMIT,
-                some,
-            )(*operands)
-            waiting.append(mod_keep)
-            far, mod_keep, mod_send = lax.optimization_barrier((far, mod_keep, mod_send))
-        far_order = [k ^ bit for k in order]
-        if bit == 1:
+        far, far_order = exchange(bit), [k ^ bit for k in order]
+        bit //= 2
+        if bit == 0:
             break
-        near = jnp.concatenate([near, far])
-        order, bit = order + far_order, bit // 2
+        near, order = jnp.concatenate([near, far]), order + far_order
     mod_other = lax.ppermute(mod_send, "segment", swap)
     weights, params = call(
         layout_kernel,

time: 36.4 us -> 37.2 us (1.022)
  waiting for transfers between devices: 12.2 us -> 14.6 us
  Pallas kernels: 10.5 us -> 8.94 us
    ppermute x3 -> x4, waiting for transfers between devices: 0.6 us -> 2.99 us  [exchange(): return lax.ppermute(near, 'space', [(i, i ^ bits) for i in range(spaces)])]
    pallas_call x2 -> x1, Pallas kernels: 4.25 us -> 2.67 us  [shards(): call(prepare_kernel, [SMEM, SMEM] + [ANY] * 5, [shape((16, width), bf16)]...]
    ppermute x3 -> x4, starting transfers between devices: 6.9 us -> 6.83 us  [exchange(): return lax.ppermute(near, 'space', [(i, i ^ bits) for i in range(spaces)])]
  transfers between devices with their start and end apart: 8 -> 9, of which waited for: 6 -> 6; matrix products, arithmetic and copies ran while one was open for 2% -> 2% of each run, Pallas kernels for 13% -> 9%
where the time goes in v3:
time: 37.2 us; the launch traced here: 36.8 us
  waiting for transfers between devices  14.6 us (39%)
  starting transfers between devices  11.1 us (30%)
  Pallas kernels  8.94 us (24%)
  other arithmetic  0.75 us (2%)
  between operations  0.72 us (2%)
  local copies, waits for them, and re-layouts  0.71 us (2%)
    ppermute x2, waiting for transfers between devices, hop(): return lax.ppermute(value, 'segment', pairs + [(b, a) for a, b in pairs])  8.59 us
    ppermute x4, starting transfers between devices, exchange(): return lax.ppermute(near, 'space', [(i, i ^ bits) for i in range(spaces)])  6.83 us
    ppermute x2, starting transfers between devices, hop(): return lax.ppermute(value, 'segment', pairs + [(b, a) for a, b in pairs])  3.66 us
    ppermute x4, waiting for transfers between devices, exchange(): return lax.ppermute(near, 'space', [(i, i ^ bits) for i in range(spaces)])  2.99 us
    pallas_call x1, Pallas kernels, shards(): call(prepare_kernel, [SMEM, SMEM] + [ANY] * 5, [shape((16, width), bf16)]...  2.67 us
    pallas_call x1, Pallas kernels, shards(): call(functools.partial(backward_kernel, sh, active, False), [VMEM] * 7, o...  2.32 us
    pallas_call x1, Pallas kernels, shards(): call(functools.partial(forward_kernel, sh, 0, (order, far_order)), [VMEM]...  2.05 us
    ppermute x1, waiting for transfers between devices, shards(): other = lax.ppermute(send, 'segment', swap)  1.63 us
  transfers between devices with their start and end apart: 9, of which 6 were waited for; matrix products, arithmetic and copies ran while one was open for 2% of the time, Pallas kernels for 9%

profile of v3, /device:TPU:0, one launch (start us, length us, event | category | flops | bytes accessed | tf_op | source)
XLA Modules:
  0.0 36.8 jit_solution(1019572895976208816)
XLA Ops:
  0.6 0.5 %collective-permute-start.4 = (bf16[2304,256]{1,0:T(8,128)(2,1)}, bf16[2304,256]{1,0:T(8,128)(2,1)S(1)}, u32[]{:S(2)}, u32[]{:S(2)}) collective-permute-start(bf16[2304,256]{1,0:T(8,128)(2,1)} %bitcast.7), channel_id=1, source_target_pairs={{0,8},{8,0},{16,24},{24,16},{1,9},{9,1},{17,25},{25,17},{2,10},{10... | collective-permute-start | bytes 3538952 | tf_op jit(solution)/shard_map/ppermute | solution.py:435
  1.2 0.7 %dynamic-slice_select_fusion = bf16[1,2,16,256]{3,2,1,0:T(8,128)(2,1)S(1)} fusion(bf16[2,2,16,256]{3,2,1,0:T(8,128)(2,1)} %param.11, s32[]{:T(128)S(6)} %select_n.27, bf16[2,2,16,256]{3,2,1,0:T(8,128)(2,1)} %param.10, pred[]{:T(512)S(6)} %eq.5), kind=kLoop, calls=%fused_computation.1 | loop fusion | flops 8192 | bytes 49157 | tf_op jit(solution)/shard_map/jit(_where)/select_n | solution.py:436
  1.9 2.7 %collective-permute-start.2 = (bf16[1,32,256]{2,1,0:T(8,128)(2,1)S(1)}, bf16[1,32,256]{2,1,0:T(8,128)(2,1)S(1)}, u32[]{:S(2)}, u32[]{:S(2)}) collective-permute-start(bf16[1,32,256]{2,1,0:T(8,128)(2,1)S(1)} %bitcast.11), channel_id=1, source_target_pairs={{0,2},{1,3},{2,0},{3,1},{4,6},{5,7},{6,4},{7,5},{8,10},{9,11},{10,... | collective-permute-start | bytes 49160 | tf_op jit(solution)/shard_map/ppermute | solution.py:453
  4.6 2.6 %collective-permute-start.1 = (bf16[1,32,256]{2,1,0:T(8,128)(2,1)S(1)}, bf16[1,32,256]{2,1,0:T(8,128)(2,1)S(1)}, u32[]{:S(2)}, u32[]{:S(2)}) collective-permute-start(bf16[1,32,256]{2,1,0:T(8,128)(2,1)S(1)} %bitcast.12), channel_id=1, source_target_pairs={{0,4},{1,5},{2,6},{3,7},{4,0},{5,1},{6,2},{7,3},{8,12},{9,13},{10,... | collective-permute-start | bytes 49160 | tf_op jit(solution)/shard_map/ppermute | solution.py:453
  7.2 0.0 collective-permute-start
  7.2 2.7 %shard_map.121 = (bf16[16,512]{1,0:T(8,128)(2,1)}, f32[8,256]{1,0:T(8,128)}, f32[8,256]{1,0:T(8,128)}) custom-call(s32[2]{0:T(128)} %times_ref.1, s32[2]{0:T(128)} %labels_ref.1, bf16[125,8,512]{2,1,0:T(8,128)(2,1)} %bitcast.9, bf16[128,512]{1,0:T(8,128)(2,1)} %refs_0_.1, bf16[512,512]{1,0:T(8,128)(2,1)} %bitcast.10, f32[1,512]{1,0:T(1,128)} %refs_2_.1, ...), custom_call_target="tpu_custom_call" | custom-call | flops 1048576 | bytes 4194304 | tf_op jit(solution)/shard_map/pallas_call | solution.py:442
  9.9 0.0 collective-permute-done.2
  9.9 2.8 %collective-permute-done = bf16[1,32,256]{2,1,0:T(8,128)(2,1)S(1)} collective-permute-done((bf16[1,32,256]{2,1,0:T(8,128)(2,1)S(1)}, bf16[1,32,256]{2,1,0:T(8,128)(2,1)S(1)}, u32[]{:S(2)}, u32[]{:S(2)}) %collective-permute-start) | collective-permute-done | bytes 16416 | tf_op jit(solution)/shard_map/ppermute | solution.py:453
  12.7 1.6 %collective-permute-start.3 = (bf16[4,32,256]{2,1,0:T(8,128)(2,1)S(1)}, bf16[4,32,256]{2,1,0:T(8,128)(2,1)S(1)}, u32[]{:S(2)}, u32[]{:S(2)}) collective-permute-start(bf16[4,32,256]{2,1,0:T(8,128)(2,1)S(1)} %pad_maximum_fusion.refs_0_), channel_id=1, source_target_pairs={{0,1},{1,0},{2,3},{3,2},{4,5},{5,4},{6,7},{7,6},{8,9},{9,8},{10,11... | collective-permute-start | bytes 196616 | tf_op jit(solution)/shard_map/ppermute | solution.py:453
  14.3 0.0 collective-permute-start.5
  14.3 1.4 %collective-permute-done.5.mod_other_any = f32[8,256]{1,0:T(8,128)S(1)} collective-permute-done((f32[8,256]{1,0:T(8,128)}, f32[8,256]{1,0:T(8,128)S(1)}, u32[]{:S(2)}, u32[]{:S(2)}) %collective-permute-start.5) | collective-permute-done | bytes 8224 | tf_op jit(solution)/shard_map/ppermute | solution.py:467
  15.7 0.0 collective-permute-done.4.other_any
  15.7 0.7 %copy-done.2 = f32[8,256]{1,0:T(8,128)S(1)} copy-done((f32[8,256]{1,0:T(8,128)S(1)}, f32[8,256]{1,0:T(8,128)}, u32[]{:S(2)}) %copy-start.2) | copy-done | bytes 8216
  16.4 0.5 %shard_map.122 = (bf16[2,2304,256]{2,1,0:T(8,128)(2,1)S(1)}, f32[8,256]{1,0:T(8,128)S(1)}) custom-call(bf16[2304,256]{1,0:T(8,128)(2,1)S(1)} %bitcast.8, bf16[2304,256]{1,0:T(8,128)(2,1)S(1)} %collective-permute-done.4.other_any, f32[8,256]{1,0:T(8,128)S(1)} %copy-done.2, f32[8,256]{1,0:T(8,128)S(1)} %collective-permute-done.5.mod_other_any), custom_call_target="tpu_custom_call" | custom-call | flops 1048576 | bytes 4194304 | tf_op jit(solution)/shard_map/pallas_call | solution.py:468
  16.9 0.2 collective-permute-done.3.refs_1_
  17.1 2.1 %shard_map.123 = (bf16[256,256]{1,0:T(8,128)(2,1)S(1)}, bf16[256,256]{1,0:T(8,128)(2,1)S(1)}, bf16[256,256]{1,0:T(8,128)(2,1)S(1)}) custom-call(bf16[4,32,256]{2,1,0:T(8,128)(2,1)S(1)} %pad_maximum_fusion.refs_0_, bf16[4,32,256]{2,1,0:T(8,128)(2,1)S(1)} %collective-permute-done.3.refs_1_, f32[8,256]{1,0:T(8,128)S(1)} %get-tuple-element.31.refs_2_.refs_3_, ...), custom_call_target="tpu_custom_call" | custom-call | tf_op jit(solution)/shard_map/pallas_call | solution.py:484
  19.1 0.1 collective-permute-start.6
  19.2 5.4 %collective-permute-done.6.refs_0_ = bf16[256,256]{1,0:T(8,128)(2,1)S(1)} collective-permute-done((bf16[256,256]{1,0:T(8,128)(2,1)S(1)}, bf16[256,256]{1,0:T(8,128)(2,1)S(1)}, u32[]{:S(2)}, u32[]{:S(2)}) %collective-permute-start.6) | collective-permute-done | bytes 131104 | tf_op jit(solution)/shard_map/ppermute | solution.py:482
  24.6 3.6 %collective-permute-start.7 = (bf16[256,256]{1,0:T(8,128)(2,1)S(1)}, bf16[256,256]{1,0:T(8,128)(2,1)S(1)}, u32[]{:S(2)}, u32[]{:S(2)}) collective-permute-start(bf16[256,256]{1,0:T(8,128)(2,1)S(1)} %get-tuple-element.36), channel_id=1, source_target_pairs={{16,0},{24,8},{0,16},{8,24},{17,1},{25,9},{1,17},{9,25},{18,2},{26... | collective-permute-start | bytes 393224 | tf_op jit(solution)/shard_map/ppermute | solution.py:482
  28.2 3.2 %collective-permute-done.7.refs_2_ = bf16[256,256]{1,0:T(8,128)(2,1)S(1)} collective-permute-done((bf16[256,256]{1,0:T(8,128)(2,1)S(1)}, bf16[256,256]{1,0:T(8,128)(2,1)S(1)}, u32[]{:S(2)}, u32[]{:S(2)}) %collective-permute-start.7) | collective-permute-done | bytes 131104 | tf_op jit(solution)/shard_map/ppermute | solution.py:482
  31.4 2.3 %shard_map.125 = (f32[328,256]{1,0:T(8,128)S(1)}, f32[328,256]{1,0:T(8,128)S(1)}) custom-call(bf16[256,256]{1,0:T(8,128)(2,1)S(1)} %get-tuple-element.33.refs_1_.refs_0_, bf16[256,256]{1,0:T(8,128)(2,1)S(1)} %get-tuple-element.34.refs_1_, bf16[256,256]{1,0:T(8,128)(2,1)S(1)} %collective-permute-done.7.refs_2_, ...), custom_call_target="tpu_custom_call", output_to_operand_aliasing={{0}: (5, {}), {1}: (6, {})} | custom-call | tf_op jit(solution)/shard_map/pallas_call | solution.py:518
  33.7 0.1 collective-permute-start.8
  33.8 1.6 %collective-permute-done.8.other_ref = f32[328,256]{1,0:T(8,128)S(1)} collective-permute-done((f32[328,256]{1,0:T(8,128)S(1)}, f32[328,256]{1,0:T(8,128)S(1)}, u32[]{:S(2)}, u32[]{:S(2)}) %collective-permute-start.8) | collective-permute-done | bytes 335904 | tf_op jit(solution)/shard_map/ppermute | solution.py:525
  35.4 1.4 %shard_map.126 = (bf16[2,32,256]{2,1,0:T(8,128)(2,1)}, f32[288,256]{1,0:T(8,128)}, f32[512,512]{1,0:T(8,128)}) custom-call(f32[328,256]{1,0:T(8,128)S(1)} %get-tuple-element.39.keep_ref, f32[328,256]{1,0:T(8,128)S(1)} %collective-permute-done.8.other_ref, bf16[16,512]{1,0:T(8,128)(2,1)S(1)} %copy-done.1, f32[1,256]{1,0:T(1,128)S(1)} %copy-done.3), custom_call_target="tpu_custom_call" | custom-call | tf_op jit(solution)/shard_map/pallas_call | solution.py:526
  (10 shorter events, 0.0 us)
Async XLA Ops:
  0.6 15.0 %copy-start = (bf16[1,3,3,256,256]{4,3,2,1,0:T(8,128)(2,1)S(1)}, bf16[1,3,3,256,256]{4,3,2,1,0:T(8,128)(2,1)}, u32[]{:S(2)}) copy-start(bf16[1,3,3,256,256]{4,3,2,1,0:T(8,128)(2,1)} %param.16) | copy-start | bytes 3538948
  0.6 15.0 %collective-permute-start.4 = (bf16[2304,256]{1,0:T(8,128)(2,1)}, bf16[2304,256]{1,0:T(8,128)(2,1)S(1)}, u32[]{:S(2)}, u32[]{:S(2)}) collective-permute-start(bf16[2304,256]{1,0:T(8,128)(2,1)} %bitcast.7), channel_id=1, source_target_pairs={{0,8},{8,0},{16,24},{24,16},{1,9},{9,1},{17,25},{25,17},{2,10},{10... | collective-permute-start | bytes 3538952 | tf_op jit(solution)/shard_map/ppermute | solution.py:435
  1.9 8.0 %collective-permute-start.2 = (bf16[1,32,256]{2,1,0:T(8,128)(2,1)S(1)}, bf16[1,32,256]{2,1,0:T(8,128)(2,1)S(1)}, u32[]{:S(2)}, u32[]{:S(2)}) collective-permute-start(bf16[1,32,256]{2,1,0:T(8,128)(2,1)S(1)} %bitcast.11), channel_id=1, source_target_pairs={{0,2},{1,3},{2,0},{3,1},{4,6},{5,7},{6,4},{7,5},{8,10},{9,11},{10,... | collective-permute-start | bytes 49160 | tf_op jit(solution)/shard_map/ppermute | solution.py:453
  4.6 5.3 %collective-permute-start.1 = (bf16[1,32,256]{2,1,0:T(8,128)(2,1)S(1)}, bf16[1,32,256]{2,1,0:T(8,128)(2,1)S(1)}, u32[]{:S(2)}, u32[]{:S(2)}) collective-permute-start(bf16[1,32,256]{2,1,0:T(8,128)(2,1)S(1)} %bitcast.12), channel_id=1, source_target_pairs={{0,4},{1,5},{2,6},{3,7},{4,0},{5,1},{6,2},{7,3},{8,12},{9,13},{10,... | collective-permute-start | bytes 49160 | tf_op jit(solution)/shard_map/ppermute | solution.py:453
  7.2 5.5 %collective-permute-start = (bf16[1,32,256]{2,1,0:T(8,128)(2,1)S(1)}, bf16[1,32,256]{2,1,0:T(8,128)(2,1)S(1)}, u32[]{:S(2)}, u32[]{:S(2)}) collective-permute-start(bf16[1,32,256]{2,1,0:T(8,128)(2,1)S(1)} %bitcast.13), channel_id=1, source_target_pairs={{0,6},{1,7},{2,4},{3,5},{4,2},{5,3},{6,0},{7,1},{8,14},{9,15},{10,... | collective-permute-start | bytes 49160 | tf_op jit(solution)/shard_map/ppermute | solution.py:453
  12.7 4.3 %collective-permute-start.3 = (bf16[4,32,256]{2,1,0:T(8,128)(2,1)S(1)}, bf16[4,32,256]{2,1,0:T(8,128)(2,1)S(1)}, u32[]{:S(2)}, u32[]{:S(2)}) collective-permute-start(bf16[4,32,256]{2,1,0:T(8,128)(2,1)S(1)} %pad_maximum_fusion.refs_0_), channel_id=1, source_target_pairs={{0,1},{1,0},{2,3},{3,2},{4,5},{5,4},{6,7},{7,6},{8,9},{9,8},{10,11... | collective-permute-start | bytes 196616 | tf_op jit(solution)/shard_map/ppermute | solution.py:453
  14.3 1.4 %collective-permute-start.5 = (f32[8,256]{1,0:T(8,128)}, f32[8,256]{1,0:T(8,128)S(1)}, u32[]{:S(2)}, u32[]{:S(2)}) collective-permute-start(f32[8,256]{1,0:T(8,128)} %get-tuple-element.30), channel_id=1, source_target_pairs={{0,8},{8,0},{16,24},{24,16},{1,9},{9,1},{17,25},{25,17},{2,10},{10... | collective-permute-start | bytes 24584 | tf_op jit(solution)/shard_map/ppermute | solution.py:467
  15.7 0.7 %copy-start.2 = (f32[8,256]{1,0:T(8,128)S(1)}, f32[8,256]{1,0:T(8,128)}, u32[]{:S(2)}) copy-start(f32[8,256]{1,0:T(8,128)} %get-tuple-element.29.mod_keep_any) | copy-start | bytes 24580
  19.1 5.5 %collective-permute-start.6 = (bf16[256,256]{1,0:T(8,128)(2,1)S(1)}, bf16[256,256]{1,0:T(8,128)(2,1)S(1)}, u32[]{:S(2)}, u32[]{:S(2)}) collective-permute-start(bf16[256,256]{1,0:T(8,128)(2,1)S(1)} %get-tuple-element.35), channel_id=1, source_target_pairs={{0,16},{8,24},{16,0},{24,8},{1,17},{9,25},{17,1},{25,9},{2,18},{10... | collective-permute-start | bytes 393224 | tf_op jit(solution)/shard_map/ppermute | solution.py:482
  24.6 6.8 %collective-permute-start.7 = (bf16[256,256]{1,0:T(8,128)(2,1)S(1)}, bf16[256,256]{1,0:T(8,128)(2,1)S(1)}, u32[]{:S(2)}, u32[]{:S(2)}) collective-permute-start(bf16[256,256]{1,0:T(8,128)(2,1)S(1)} %get-tuple-element.36), channel_id=1, source_target_pairs={{16,0},{24,8},{0,16},{8,24},{17,1},{25,9},{1,17},{9,25},{18,2},{26... | collective-permute-start | bytes 393224 | tf_op jit(solution)/shard_map/ppermute | solution.py:482
  31.4 4.0 %copy-start.1 = (bf16[16,512]{1,0:T(8,128)(2,1)S(1)}, bf16[16,512]{1,0:T(8,128)(2,1)}, u32[]{:S(2)}) copy-start(bf16[16,512]{1,0:T(8,128)(2,1)} %get-tuple-element.41.embedded_ref) | copy-start | bytes 49156
  31.4 4.0 %copy-start.3 = (f32[1,256]{1,0:T(1,128)S(1)}, f32[1,256]{1,0:T(1,128)}, u32[]{:S(2)}) copy-start(f32[1,256]{1,0:T(1,128)} %gain_ref.1) | copy-start | bytes 3076
  33.7 1.7 %collective-permute-start.8 = (f32[328,256]{1,0:T(8,128)S(1)}, f32[328,256]{1,0:T(8,128)S(1)}, u32[]{:S(2)}, u32[]{:S(2)}) collective-permute-start(f32[328,256]{1,0:T(8,128)S(1)} %get-tuple-element.40), channel_id=1, source_target_pairs={{0,8},{8,0},{16,24},{24,16},{1,9},{9,1},{17,25},{25,17},{2,10},{10... | collective-permute-start | bytes 1007624 | tf_op jit(solution)/shard_map/ppermute | solution.py:525
